TPU v7x, 32 devices: a whole 2x2x4 slice. The times are simulated.
32 devices in a mesh: ep: 16 (over z, y, core), dp: 2 (over x).
Axes of the slice: x: 2, y: 2, z: 4, core: 2. Of those that a mesh axis runs over, the one named last changes fastest.
Arguments:
- tokens: bfloat16 [128, 7168], P('ep', 'dp'), may hold values from -6 to 6
- cotangent: bfloat16 [128, 7168], P('ep', 'dp'), may hold values from -6 to 6
- routes: int32 [128, 8], P('ep'), may hold values from 0 to 15, all different within a row; in each aligned block of 8 rows (0 to 7, 8 to 15, ...) at most 8 rows name the same one
- route_weights: float32 [128, 8], P('ep'), may hold values from 0.05 to 0.5
- gate_up: bfloat16 [16, 7168, 4096], P('ep', 'dp'), may hold values from -0.0625 to 0.0625
- down_proj: bfloat16 [16, 2048, 7168], P('ep', None, 'dp'), may hold values from -0.125 to 0.125
Outputs:
- mixed: bfloat16 [128, 7168], P('ep', 'dp')
- token_grad: bfloat16 [128, 7168], P('ep', 'dp')
- gate_up_grad: bfloat16 [16, 7168, 4096], P('ep', 'dp')
Inputs may be any that keep to these rules, and one draw needn't show every extreme that they name: `routes`: each token names 8 different experts. The 8 tokens of one index of ep (aligned blocks of rows) name any one expert at most 8 times, a bound that some block reaches.
All inputs are finite; a program needn't handle non-finite values.
Results may differ from a plain program's by a relative error of at most 0.015.
Values may be sent and summed in bfloat16 or wider, within the bound.
A program may use at most 192 MiB of HBM per device.

v0:
```python
import jax
import jax.numpy as jnp
from jax import lax
from jax.sharding import PartitionSpec as P

FF = 2048


def on_device(tokens, cotangent, routes, route_weights, gate_up, down_proj):
    tok_rows = tokens.shape[0]
    width = tokens.shape[1]
    chosen = routes.shape[1]
    hidden_units = down_proj.shape[1]
    split = FF // hidden_units
    ep_count = lax.axis_size("ep")
    experts = ep_count // split
    capacity = min(tok_rows, max(2, 2 * chosen * tok_rows // experts))
    slot_count = experts * capacity
    pair_count = tok_rows * chosen
    flat_routes = routes.reshape(-1)
    order = jnp.arange(pair_count, dtype=jnp.int32)
    earlier = order[None, :] < order[:, None]
    same = flat_routes[:, None] == flat_routes[None, :]
    rank_of = jnp.sum((same & earlier).astype(jnp.int32), axis=1)
    slot_ids = flat_routes * capacity + rank_of
    hits = (slot_ids[:, None] == jnp.arange(slot_count, dtype=jnp.int32)[None, :]).astype(
        jnp.float32
    )
    hits = hits.reshape(tok_rows, chosen, slot_count)
    token_slots = jnp.sum(hits, axis=1)
    weighted_slots = jnp.sum(hits * route_weights[:, :, None], axis=1)
    x_send = lax.dot_general(
        token_slots.astype(jnp.bfloat16),
        tokens,
        (((0,), (0,)), ((), ())),
        preferred_element_type=jnp.float32,
    ).astype(jnp.bfloat16)
    d_send = lax.dot_general(
        weighted_slots,
        cotangent.astype(jnp.float32),
        (((0,), (0,)), ((), ())),
        precision=lax.Precision.HIGHEST,
        preferred_element_type=jnp.float32,
    ).astype(jnp.bfloat16)
    x_wide = jnp.broadcast_to(
        x_send.reshape(experts, 1, capacity, width), (experts, split, capacity, width)
    ).reshape(ep_count, capacity, width)
    d_wide = jnp.broadcast_to(
        d_send.reshape(experts, 1, capacity, width), (experts, split, capacity, width)
    ).reshape(ep_count, capacity, width)
    x_recv, d_recv = (
        lax.all_to_all(x_wide, "ep", split_axis=0, concat_axis=0, tiled=True),
        lax.all_to_all(d_wide, "ep", split_axis=0, concat_axis=0, tiled=True),
    )
    row_count = ep_count * capacity
    x_rows = x_recv.reshape(row_count, width)
    d_rows = d_recv.reshape(row_count, width)
    w_pair = gate_up[0]
    w_down = down_proj[0]
    partial_pre = jnp.dot(x_rows, w_pair, preferred_element_type=jnp.float32)
    partial_back = lax.dot_general(
        d_rows, w_down, (((1,), (1,)), ((), ())), preferred_element_type=jnp.float32
    )
    pre, grad_hidden = (
        lax.psum(partial_pre.astype(jnp.bfloat16), "dp").astype(jnp.float32),
        lax.psum(partial_back.astype(jnp.bfloat16), "dp").astype(jnp.float32),
    )
    gate = pre[:, :hidden_units]
    upper = pre[:, hidden_units:]
    sigmoid_g = jax.nn.sigmoid(gate)
    silu_g = gate * sigmoid_g
    hidden = (silu_g * upper).astype(jnp.bfloat16)
    grad_gate = (grad_hidden * upper * sigmoid_g * (1.0 + gate * (1.0 - sigmoid_g))).astype(
        jnp.bfloat16
    )
    grad_up = (grad_hidden * silu_g).astype(jnp.bfloat16)
    grad_pair = jnp.concatenate([grad_gate, grad_up], axis=1)
    out_rows = jnp.dot(hidden, w_down, preferred_element_type=jnp.float32).astype(jnp.bfloat16)
    weight_grad = lax.dot_general(
        x_rows, grad_pair, (((0,), (0,)), ((), ())), preferred_element_type=jnp.float32
    ).astype(jnp.bfloat16)
    dx_rows = lax.dot_general(
        grad_pair, w_pair, (((1,), (1,)), ((), ())), preferred_element_type=jnp.float32
    ).astype(jnp.bfloat16)
    out_back, dx_back = (
        lax.all_to_all(
            out_rows.reshape(ep_count, capacity, width),
            "ep",
            split_axis=0,
            concat_axis=0,
            tiled=True,
        ),
        lax.all_to_all(
            dx_rows.reshape(ep_count, capacity, width),
            "ep",
            split_axis=0,
            concat_axis=0,
            tiled=True,
        ),
    )
    out_total = jnp.sum(
        out_back.astype(jnp.float32).reshape(experts, split, capacity, width), axis=1
    ).reshape(slot_count, width)
    dx_total = jnp.sum(
        dx_back.astype(jnp.float32).reshape(experts, split, capacity, width), axis=1
    ).reshape(slot_count, width)
    mixed = jnp.dot(
        weighted_slots,
        out_total,
        precision=lax.Precision.HIGHEST,
        preferred_element_type=jnp.float32,
    ).astype(jnp.bfloat16)
    token_grad = jnp.dot(
        token_slots, dx_total, precision=lax.Precision.HIGHEST, preferred_element_type=jnp.float32
    ).astype(jnp.bfloat16)
    return (mixed, token_grad, weight_grad[None])


def solution(mesh):
    return jax.shard_map(
        on_device,
        mesh=mesh,
        in_specs=(
            P("ep", "dp"),
            P("ep", "dp"),
            P("ep", None),
            P("ep", None),
            P("ep", "dp", None),
            P("ep", None, "dp"),
        ),
        out_specs=(P("ep", "dp"), P("ep", "dp"), P("ep", "dp", None)),
        check_vma=False,
    )
```

profile of v0, /device:TPU:0, one launch (start us, length us, event | category | flops | bytes accessed | tf_op | source)
XLA Modules:
  0.0 204.0 jit_solution(1491191971874056628)
XLA Ops:
  7.2 0.0 copy-start
  7.2 0.8 eq.29
  8.0 0.2 convert_reduce_fusion.1
  8.1 0.1 reduce_sum.30
  8.2 0.7 multiply_add_fusion
  8.9 0.8 convert_reduce_fusion
  9.7 1.9 fusion.19
  11.6 7.4 %all-to-all-start.2 = ((bf16[16,8,3584]{2,1,0:T(8,128)(2,1)}), bf16[16,8,3584]{2,1,0:T(8,128)(2,1)S(1)}, u32[]{:S(2)}, u32[]{:S(2)}) async-start(bf16[16,8,3584]{2,1,0:T(8,128)(2,1)} %fusion.19), calls=%async_computation.2 | async-start | bytes 1835008 | tf_op jit(solution)/shard_map/all_to_all | solution.py:53
  19.0 2.2 %fusion.18 = bf16[16,8,3584]{2,1,0:T(8,128)(2,1)} fusion(bf16[8,3584]{1,0:T(8,128)(2,1)} %param.6, f32[8,128]{1,0:T(8,128)S(1)} %get-tuple-element.3), kind=kOutput, calls=%fused_computation.15 | convolution fusion | flops 7799808 | bytes 978944 | tf_op jit(solution)/shard_map/dot_general | solution.py:32
  21.2 18.6 %all-to-all-done.2 = bf16[16,8,3584]{2,1,0:T(8,128)(2,1)S(1)} async-done(((bf16[16,8,3584]{2,1,0:T(8,128)(2,1)}), bf16[16,8,3584]{2,1,0:T(8,128)(2,1)S(1)}, u32[]{:S(2)}, u32[]{:S(2)}) %all-to-all-start.2) | async-done | bytes 917536 | tf_op jit(solution)/shard_map/all_to_all | solution.py:53
  39.8 6.2 %all-to-all-start = ((bf16[16,8,3584]{2,1,0:T(8,128)(2,1)}), bf16[16,8,3584]{2,1,0:T(8,128)(2,1)S(1)}, u32[]{:S(2)}, u32[]{:S(2)}) async-start(bf16[16,8,3584]{2,1,0:T(8,128)(2,1)} %fusion.18), calls=%async_computation | async-start | bytes 1835008 | tf_op jit(solution)/shard_map/all_to_all | solution.py:52
  46.0 0.0 all-reduce.3.cloned.1.call-start
  46.0 10.7 %fusion.26 = bf16[128,2048]{1,0:T(8,128)(2,1)} fusion(bf16[1,2048,3584]{2,1,0:T(8,128)(2,1)} %param.11, bf16[16,8,3584]{2,1,0:T(8,128)(2,1)S(1)} %all-to-all-done.2), kind=kOutput, calls=%fused_computation.21 | convolution fusion | flops 1879310336 | bytes 16121856 | tf_op jit(solution)/shard_map/dot_general | solution.py:61
  56.7 10.1 %all-to-all-done = bf16[16,8,3584]{2,1,0:T(8,128)(2,1)S(1)} async-done(((bf16[16,8,3584]{2,1,0:T(8,128)(2,1)}), bf16[16,8,3584]{2,1,0:T(8,128)(2,1)S(1)}, u32[]{:S(2)}, u32[]{:S(2)}) %all-to-all-start) | async-done | bytes 917536 | tf_op jit(solution)/shard_map/all_to_all | solution.py:52
  66.8 12.7 %fusion.12 = bf16[128,4096]{1,0:T(8,128)(2,1)} fusion(bf16[1,3584,4096]{2,1,0:T(8,128)(2,1)} %param.10, bf16[16,8,3584]{2,1,0:T(8,128)(2,1)S(1)} %all-to-all-done), kind=kOutput, calls=%fused_computation.11 | convolution fusion | flops 3758620672 | bytes 31326208 | tf_op jit(solution)/shard_map/dot_general | solution.py:60
  79.5 0.0 all-reduce.3.cloned.1.call-update
  79.5 53.3 %all-reduce.3.cloned.1.call-done = (bf16[128,4096]{1,0:T(8,128)(2,1)}, bf16[128,2048]{1,0:T(8,128)(2,1)}) async-done(((bf16[128,4096]{1,0:T(8,128)(2,1)}, bf16[128,2048]{1,0:T(8,128)(2,1)}), (bf16[128,4096]{1,0:T(8,128)(2,1)}, bf16[128,2048]{1,0:T(8,128)(2,1)})) %all-reduce.3.cloned.1.call-update) | async-done | bytes 1572880 | tf_op jit(solution)/shard_map/psum | solution.py:65
  132.8 1.4 convert_element_type.60
  134.2 8.3 %fusion.23 = bf16[16,8,3584]{2,1,0:T(8,128)(2,1)} fusion(bf16[1,2048,3584]{2,1,0:T(8,128)(2,1)} %param.11, f32[128,4096]{1,0:T(8,128)S(1)} %convert_element_type.60), kind=kOutput, calls=%fused_computation.18 | convolution fusion | flops 1881079808 | bytes 17694720 | tf_op jit(solution)/shard_map/dot_general | solution.py:78
  142.5 5.7 %all-to-all-start.1 = ((bf16[16,8,3584]{2,1,0:T(8,128)(2,1)}), bf16[16,8,3584]{2,1,0:T(8,128)(2,1)}, u32[]{:S(2)}, u32[]{:S(2)}) async-start(bf16[16,8,3584]{2,1,0:T(8,128)(2,1)} %fusion.23), calls=%async_computation.1 | async-start | bytes 1835008 | tf_op jit(solution)/shard_map/all_to_all | solution.py:86
  148.2 1.6 fusion.31
  149.8 0.8 copy-done.2
  150.6 0.2 copy-done.3
  150.8 15.2 %fusion.20 = bf16[16,8,3584]{2,1,0:T(8,128)(2,1)} fusion(bf16[1,3584,4096]{2,1,0:T(8,128)(2,1)} %param.10, bf16[128,2048]{1,0:T(8,128)(2,1)S(1)} %get-tuple-element.8, bf16[128,2048]{1,0:T(8,128)(2,1)S(1)} %get-tuple-element.7), kind=kOutput, calls=%fused_computation.17 | convolution fusion | flops 3760652288 | bytes 31326208 | tf_op jit(solution)/shard_map/dot_general | solution.py:82
  166.0 3.1 %all-to-all-done.1 = bf16[16,8,3584]{2,1,0:T(8,128)(2,1)} async-done(((bf16[16,8,3584]{2,1,0:T(8,128)(2,1)}), bf16[16,8,3584]{2,1,0:T(8,128)(2,1)}, u32[]{:S(2)}, u32[]{:S(2)}) %all-to-all-start.1) | async-done | bytes 917536 | tf_op jit(solution)/shard_map/all_to_all | solution.py:86
  169.1 6.2 %all-to-all-start.3 = ((bf16[16,8,3584]{2,1,0:T(8,128)(2,1)}), bf16[16,8,3584]{2,1,0:T(8,128)(2,1)S(1)}, u32[]{:S(2)}, u32[]{:S(2)}) async-start(bf16[16,8,3584]{2,1,0:T(8,128)(2,1)} %fusion.20), calls=%async_computation.3 | async-start | bytes 1835008 | tf_op jit(solution)/shard_map/all_to_all | solution.py:93
  175.3 0.0 copy-start.1
  175.3 15.5 %fusion.4 = bf16[1,3584,4096]{2,1,0:T(8,128)(2,1)} fusion(bf16[16,8,3584]{2,1,0:T(8,128)(2,1)S(1)} %all-to-all-done, bf16[128,2048]{1,0:T(8,128)(2,1)} %copy-done.3, bf16[128,2048]{1,0:T(8,128)(2,1)} %copy-done.2), kind=kOutput, calls=%fused_computation.5 | convolution fusion | flops 3774873600 | bytes 31326208 | tf_op jit(solution)/shard_map/dot_general | solution.py:79
  190.8 2.3 %convolution_convert_fusion.4 = bf16[8,3584]{1,0:T(8,128)(2,1)} fusion(f32[8,128]{1,0:T(8,128)S(1)} %get-tuple-element.4, bf16[16,8,3584]{2,1,0:T(8,128)(2,1)} %all-to-all-done.1), kind=kOutput, calls=%fused_computation.20 | convolution fusion | flops 44068864 | bytes 978944 | tf_op jit(solution)/shard_map/dot_general | solution.py:107
  193.1 3.0 %all-to-all-done.3 = bf16[16,8,3584]{2,1,0:T(8,128)(2,1)S(1)} async-done(((bf16[16,8,3584]{2,1,0:T(8,128)(2,1)}), bf16[16,8,3584]{2,1,0:T(8,128)(2,1)S(1)}, u32[]{:S(2)}, u32[]{:S(2)}) %all-to-all-start.3) | async-done | bytes 917536 | tf_op jit(solution)/shard_map/all_to_all | solution.py:93
  196.1 1.1 convolution_convert_fusion.3
  197.2 0.0 copy-done.1
  (3 shorter events, 0.0 us)
Async XLA Ops:
  7.2 2.6 %copy-start = (bf16[8,3584]{1,0:T(8,128)(2,1)S(1)}, bf16[8,3584]{1,0:T(8,128)(2,1)}, u32[]{:S(2)}) copy-start(bf16[8,3584]{1,0:T(8,128)(2,1)} %param.7) | copy-start | bytes 172036
  11.6 28.2 %all-to-all-start.2 = ((bf16[16,8,3584]{2,1,0:T(8,128)(2,1)}), bf16[16,8,3584]{2,1,0:T(8,128)(2,1)S(1)}, u32[]{:S(2)}, u32[]{:S(2)}) async-start(bf16[16,8,3584]{2,1,0:T(8,128)(2,1)} %fusion.19), calls=%async_computation.2 | async-start | bytes 1835008 | tf_op jit(solution)/shard_map/all_to_all | solution.py:53
  39.8 27.0 %all-to-all-start = ((bf16[16,8,3584]{2,1,0:T(8,128)(2,1)}), bf16[16,8,3584]{2,1,0:T(8,128)(2,1)S(1)}, u32[]{:S(2)}, u32[]{:S(2)}) async-start(bf16[16,8,3584]{2,1,0:T(8,128)(2,1)} %fusion.18), calls=%async_computation | async-start | bytes 1835008 | tf_op jit(solution)/shard_map/all_to_all | solution.py:52
  46.0 86.8 %all-reduce.3.cloned.1.call-start = ((), (), s32[]{:S(2)}) async-start(), calls=%async_computation.4 | async-start | bytes 3145728 | tf_op jit(solution)/shard_map/psum | solution.py:65
  142.5 26.5 %all-to-all-start.1 = ((bf16[16,8,3584]{2,1,0:T(8,128)(2,1)}), bf16[16,8,3584]{2,1,0:T(8,128)(2,1)}, u32[]{:S(2)}, u32[]{:S(2)}) async-start(bf16[16,8,3584]{2,1,0:T(8,128)(2,1)} %fusion.23), calls=%async_computation.1 | async-start | bytes 1835008 | tf_op jit(solution)/shard_map/all_to_all | solution.py:86
  149.8 0.8 copy-start.2
  149.8 1.0 copy-start.3
  169.1 27.0 %all-to-all-start.3 = ((bf16[16,8,3584]{2,1,0:T(8,128)(2,1)}), bf16[16,8,3584]{2,1,0:T(8,128)(2,1)S(1)}, u32[]{:S(2)}, u32[]{:S(2)}) async-start(bf16[16,8,3584]{2,1,0:T(8,128)(2,1)} %fusion.20), calls=%async_computation.3 | async-start | bytes 1835008 | tf_op jit(solution)/shard_map/all_to_all | solution.py:93
  175.3 21.9 %copy-start.1 = (bf16[8,3584]{1,0:T(8,128)(2,1)S(1)}, bf16[8,3584]{1,0:T(8,128)(2,1)}, u32[]{:S(2)}) copy-start(bf16[8,3584]{1,0:T(8,128)(2,1)} %param.7) | copy-start | bytes 172036
Sparse Core Ops, SparseCore 0:
  79.6 53.1 all-reduce.2
where the time goes:
time: 205 us; the launch traced here: 204 us
  waiting for transfers between devices  88.1 us (43%)
  matrix products  69.8 us (34%)
  starting transfers between devices  25.4 us (12%)
  between operations  14.1 us (7%)
  other arithmetic  4.69 us (2%)
    psum x1, waiting for transfers between devices, on_device(): lax.psum(partial_pre.astype(jnp.bfloat16), 'dp').astype(jnp.float32)  53.3 us
    all_to_all x1, waiting for transfers between devices, on_device(): lax.all_to_all(d_wide, 'ep', split_axis=0, concat_axis=0, tiled=True)  18.6 us
    dot_general x1, matrix products, on_device(): lax.dot_general(x_rows, grad_pair, (((0,), (0,)), ((), ())), preferred_el...  15.5 us
    dot_general x1, matrix products, on_device(): lax.dot_general(grad_pair, w_pair, (((1,), (1,)), ((), ())), preferred_el...  15.2 us
    dot_general x1, matrix products, on_device(): partial_pre = jnp.dot(x_rows, w_pair, preferred_element_type=jnp.float32)  12.7 us
    dot_general x1, matrix products, on_device(): lax.dot_general(d_rows, w_down, (((1,), (1,)), ((), ())), preferred_eleme...  10.7 us
    all_to_all x1, waiting for transfers between devices, on_device(): lax.all_to_all(x_wide, 'ep', split_axis=0, concat_axis=0, tiled=True)  10.1 us
    dot_general x1, matrix products, on_device(): jnp.dot(hidden, w_down, preferred_element_type=jnp.float32)  8.28 us
  transfers between devices with their start and end apart: 5, of which 5 were waited for; matrix products, arithmetic and copies ran while one was open for 23% of the time, Pallas kernels for 0%

commit v1 on v0

v1 whole, which is shorter than its diff:
```python
import jax
import jax.numpy as jnp
from jax import lax
from jax.sharding import PartitionSpec as P

FF = 2048
PIECE = 1024


def dp_sum(part, dp_count):
    sent = part.astype(jnp.bfloat16)
    if dp_count != 2:
        return lax.psum(sent, "dp").astype(jnp.float32)
    other = lax.ppermute(sent, "dp", [(0, 1), (1, 0)])
    return sent.astype(jnp.float32) + other.astype(jnp.float32)


def on_device(tokens, cotangent, routes, route_weights, gate_up, down_proj):
    tok_rows, width = tokens.shape
    hidden_units = down_proj.shape[1]
    split = FF // hidden_units
    ep_count = lax.axis_size("ep")
    dp_count = lax.axis_size("dp")
    experts = ep_count // split
    expert = lax.axis_index("ep") // split
    table = jnp.sum(
        jnp.where(
            routes[:, :, None] == jnp.arange(experts, dtype=jnp.int32)[None, None, :],
            route_weights[:, :, None],
            0.0,
        ),
        axis=1,
    )
    high = lax.reduce_precision(table, 8, 7)
    rest = table - high
    middle = lax.reduce_precision(rest, 8, 7)
    low = rest - middle
    packed = jnp.concatenate([high, middle, low], axis=1).astype(jnp.bfloat16)
    packed = jnp.pad(packed, ((0, 0), (0, -packed.shape[1] % 128)))
    first = lax.all_gather(jnp.concatenate([tokens, packed], axis=1), "ep", axis=0, tiled=True)
    d_all = lax.all_gather(cotangent, "ep", axis=0, tiled=True)
    x_all = first[:, :width]
    parts = first[:, width:].astype(jnp.float32)
    mine = jnp.arange(experts, dtype=jnp.int32)[None, :] == expert
    weight = jnp.sum(
        jnp.where(
            mine,
            parts[:, :experts]
            + (parts[:, experts : 2 * experts] + parts[:, 2 * experts : 3 * experts]),
            0.0,
        ),
        axis=1,
        keepdims=True,
    )
    named = weight > 0.0
    x_rows = jnp.where(named, x_all, jnp.zeros_like(x_all))
    d_rows = (weight * d_all.astype(jnp.float32)).astype(jnp.bfloat16)
    w_pair = gate_up[0]
    w_down = down_proj[0]
    piece = min(PIECE, hidden_units)
    pre = [
        dp_sum(
            jnp.dot(x_rows, w_pair[:, at : at + piece], preferred_element_type=jnp.float32),
            dp_count,
        )
        for at in range(0, 2 * hidden_units, piece)
    ]
    back = [
        dp_sum(
            lax.dot_general(
                d_rows,
                w_down[at : at + piece],
                (((1,), (1,)), ((), ())),
                preferred_element_type=jnp.float32,
            ),
            dp_count,
        )
        for at in range(0, hidden_units, piece)
    ]
    gate = jnp.concatenate(pre[: len(back)], axis=1)
    upper = jnp.concatenate(pre[len(back) :], axis=1)
    grad_hidden = jnp.concatenate(back, axis=1)
    sigmoid_g = jax.nn.sigmoid(gate)
    silu_g = gate * sigmoid_g
    hidden = (silu_g * upper).astype(jnp.bfloat16)
    grad_gate = (grad_hidden * upper * sigmoid_g * (1.0 + gate * (1.0 - sigmoid_g))).astype(
        jnp.bfloat16
    )
    grad_up = (grad_hidden * silu_g).astype(jnp.bfloat16)
    grad_pair = jnp.concatenate([grad_gate, grad_up], axis=1)
    out_rows = (weight * jnp.dot(hidden, w_down, preferred_element_type=jnp.float32)).astype(
        jnp.bfloat16
    )
    mixed = lax.psum_scatter(out_rows, "ep", scatter_dimension=0, tiled=True)
    dx_rows = lax.dot_general(
        grad_pair, w_pair, (((1,), (1,)), ((), ())), preferred_element_type=jnp.float32
    ).astype(jnp.bfloat16)
    token_grad = lax.psum_scatter(dx_rows, "ep", scatter_dimension=0, tiled=True)
    weight_grad = lax.dot_general(
        x_rows, grad_pair, (((0,), (0,)), ((), ())), preferred_element_type=jnp.float32
    ).astype(jnp.bfloat16)
    return (mixed, token_grad, weight_grad[None])


def solution(mesh):
    return jax.shard_map(
        on_device,
        mesh=mesh,
        in_specs=(
            P("ep", "dp"),
            P("ep", "dp"),
            P("ep", None),
            P("ep", None),
            P("ep", "dp", None),
            P("ep", None, "dp"),
        ),
        out_specs=(P("ep", "dp"), P("ep", "dp"), P("ep", "dp", None)),
        check_vma=False,
    )
```

time: 205 us -> 213 us (1.039)
  blocking collectives: 0 us -> 45.9 us
  starting transfers between devices: 25.4 us -> 6.75 us
  matrix products: 69.8 us -> 55.8 us
  waiting for transfers between devices: 88.1 us -> 83.8 us
    reduce_scatter x0 -> x2, waiting for transfers between devices: none -> 79.7 us  [the longest x1 60.7 us: on_device(): lax.psum_scatter(dx_rows, 'ep', scatter_dimension=0, tiled=True)]
    psum x1 -> x0, waiting for transfers between devices: 53.3 us -> none  [on_device(): lax.psum(partial_pre.astype(jnp.bfloat16), 'dp').astype(jnp.float32)]
    all_gather x0 -> x2, blocking collectives: none -> 45.9 us  [the longest x1 25.9 us: on_device(): lax.all_gather(jnp.concatenate([tokens, packed], axis=1), 'ep', axis=0, t...]
    all_to_all x4 -> x0, waiting for transfers between devices: 34.8 us -> none  [the longest x1 18.6 us: on_device(): lax.all_to_all(d_wide, 'ep', split_axis=0, concat_axis=0, tiled=True)]
    all_to_all x4 -> x0, starting transfers between devices: 25.4 us -> none  [the longest x1 7.38 us: on_device(): lax.all_to_all(d_wide, 'ep', split_axis=0, concat_axis=0, tiled=True)]
    dot_general x6, matrix products: 30.8 us -> 22.6 us  [the longest x4 17.5 us: on_device(): jnp.dot(x_rows, w_pair[:, at:at + piece], preferred_element_type=jnp.floa...]
    ppermute x0 -> x6, starting transfers between devices: none -> 6.49 us  [dp_sum(): other = lax.ppermute(sent, 'dp', [(0, 1), (1, 0)])]
    dot_general x1, matrix products: 8.28 us -> 3.31 us  [on_device(): jnp.dot(hidden, w_down, preferred_element_type=jnp.float32)]
  transfers between devices with their start and end apart: 5 -> 8, of which waited for: 5 -> 3; matrix products, arithmetic and copies ran while one was open for 23% -> 25% of each run, Pallas kernels for 0% -> 0%
where the time goes in v1:
time: 213 us; the launch traced here: 212 us
  waiting for transfers between devices  83.8 us (39%)
  matrix products  55.8 us (26%)
  blocking collectives  45.9 us (22%)
  between operations  14.3 us (7%)
  starting transfers between devices  6.75 us (3%)
  other arithmetic  4.04 us (2%)
    reduce_scatter x1, waiting for transfers between devices, on_device(): lax.psum_scatter(dx_rows, 'ep', scatter_dimension=0, tiled=True)  60.7 us
    all_gather x1, blocking collectives, on_device(): lax.all_gather(jnp.concatenate([tokens, packed], axis=1), 'ep', axis=0, t...  25.9 us
    all_gather x1, blocking collectives, on_device(): d_all = lax.all_gather(cotangent, 'ep', axis=0, tiled=True)  20.1 us
    reduce_scatter x1, waiting for transfers between devices, on_device(): mixed = lax.psum_scatter(out_rows, 'ep', scatter_dimension=0, tiled=True)  19 us
    dot_general x4, matrix products, on_device(): jnp.dot(x_rows, w_pair[:, at:at + piece], preferred_element_type=jnp.floa...  17.5 us
    dot_general x1, matrix products, on_device(): lax.dot_general(grad_pair, w_pair, (((1,), (1,)), ((), ())), preferred_el...  15.5 us
    dot_general x1, matrix products, on_device(): lax.dot_general(x_rows, grad_pair, (((0,), (0,)), ((), ())), preferred_el...  14.4 us
    ppermute x6, starting transfers between devices, dp_sum(): other = lax.ppermute(sent, 'dp', [(0, 1), (1, 0)])  6.49 us
  transfers between devices with their start and end apart: 8, of which 3 were waited for; matrix products, arithmetic and copies ran while one was open for 25% of the time, Pallas kernels for 0%

profile of v1, /device:TPU:0, one launch (start us, length us, event | category | flops | bytes accessed | tf_op | source)
XLA Modules:
  0.0 212.2 jit_solution(9090986752854167870)
XLA Ops:
  7.2 0.8 select_reduce_fusion
  8.0 0.1 fusion.50
  8.1 0.8 pad_maximum_fusion.6
  8.9 25.9 %all_gather.6 = bf16[128,3712]{1,0:T(8,128)(2,1)S(1)} all-gather(bf16[8,3712]{1,0:T(8,128)(2,1)S(1)} %pad_maximum_fusion.6), channel_id=1, replica_groups=mesh['ep'=16,'dp'=2] {'ep'}, dimensions={0}, use_global_device_ids=true | all-gather | bytes 1009664 | tf_op jit(solution)/shard_map/all_gather | solution.py:40
  34.8 0.2 fusion.44
  35.0 4.3 %fusion.29 = bf16[128,1024]{1,0:T(8,128)(2,1)S(1)} fusion(bf16[3584,4096]{1,0:T(8,128)(2,1)} %bitcast.22, bf16[128,3712]{1,0:T(8,128)(2,1)S(1)} %all_gather.6, pred[128]{0:T(512)(128)(4,1)S(1)} %broadcast_compare_fusion), kind=kOutput, calls=%fused_computation.24 | convolution fusion | flops 940113920 | bytes 8520192 | tf_op jit(solution)/shard_map/dot_general | solution.py:63
  39.3 1.6 collective-permute-start
  40.8 4.4 %fusion.38 = bf16[128,1024]{1,0:T(8,128)(2,1)S(1)} fusion(bf16[3584,4096]{1,0:T(8,128)(2,1)} %bitcast.23, bf16[128,3712]{1,0:T(8,128)(2,1)S(1)} %all_gather.6, pred[128]{0:T(512)(128)(4,1)S(1)} %broadcast_compare_fusion), kind=kOutput, calls=%fused_computation.27 | convolution fusion | flops 940113920 | bytes 8520192 | tf_op jit(solution)/shard_map/dot_general | solution.py:63
  45.3 0.6 collective-permute-start.3
  45.9 4.7 %fusion.35 = bf16[128,1024]{1,0:T(8,128)(2,1)S(1)} fusion(bf16[3584,4096]{1,0:T(8,128)(2,1)} %bitcast.24, bf16[128,3712]{1,0:T(8,128)(2,1)S(1)} %all_gather.6, pred[128]{0:T(512)(128)(4,1)S(1)} %broadcast_compare_fusion), kind=kOutput, calls=%fused_computation.26 | convolution fusion | flops 940113920 | bytes 8520192 | tf_op jit(solution)/shard_map/dot_general | solution.py:63
  50.6 1.1 collective-permute-start.2
  51.7 4.2 %fusion.32 = bf16[128,1024]{1,0:T(8,128)(2,1)S(1)} fusion(bf16[3584,4096]{1,0:T(8,128)(2,1)} %bitcast.25, bf16[128,3712]{1,0:T(8,128)(2,1)S(1)} %all_gather.6, pred[128]{0:T(512)(128)(4,1)S(1)} %broadcast_compare_fusion), kind=kOutput, calls=%fused_computation.25 | convolution fusion | flops 940113920 | bytes 8520192 | tf_op jit(solution)/shard_map/dot_general | solution.py:63
  55.9 1.0 collective-permute-start.1
  57.0 20.1 %all_gather.7 = bf16[128,3584]{1,0:T(8,128)(2,1)S(1)} all-gather(bf16[8,3584]{1,0:T(8,128)(2,1)S(1)} %copy-done.2), channel_id=1, replica_groups=mesh['ep'=16,'dp'=2] {'ep'}, dimensions={0}, use_global_device_ids=true | all-gather | bytes 974848 | tf_op jit(solution)/shard_map/all_gather | solution.py:41
  77.1 2.5 %fusion.23 = bf16[128,1024]{1,0:T(8,128)(2,1)S(1)} fusion(bf16[1,2048,3584]{2,1,0:T(8,128)(2,1)S(1)} %bitcast.27, bf16[128,3584]{1,0:T(8,128)(2,1)S(1)} %all_gather.7, f32[128]{0:T(128)S(1)} %fusion.44), kind=kOutput, calls=%fused_computation.22 | convolution fusion | flops 941031424 | bytes 8520192 | tf_op jit(solution)/shard_map/dot_general | solution.py:70
  79.6 1.2 collective-permute-start.4
  80.8 2.5 %fusion.26 = bf16[128,1024]{1,0:T(8,128)(2,1)S(1)} fusion(bf16[1,2048,3584]{2,1,0:T(8,128)(2,1)S(1)} %bitcast.27, bf16[128,3584]{1,0:T(8,128)(2,1)S(1)} %all_gather.7, f32[128]{0:T(128)S(1)} %fusion.44), kind=kOutput, calls=%fused_computation.23 | convolution fusion | flops 941031424 | bytes 8520192 | tf_op jit(solution)/shard_map/dot_general | solution.py:70
  83.4 0.9 collective-permute-start.5
  84.4 0.1 convert_add_fusion.2
  84.4 0.1 convert_add_fusion.3
  84.5 0.1 convert_add_fusion.4
  84.6 0.7 copy-done
  85.3 0.8 copy-done.1
  86.1 3.3 %fusion.20 = bf16[128,3584]{1,0:T(8,128)(2,1)} fusion(bf16[1,2048,3584]{2,1,0:T(8,128)(2,1)S(1)} %bitcast.27, f32[128]{0:T(128)S(1)} %fusion.44, f32[128,1024]{1,0:T(8,128)S(1)} %convert_add_fusion.2, f32[128,1024]{1,0:T(8,128)S(1)} %convert_add_fusion.3, f32[128,1024]{1,0:T(8,128)S(1)} %convert_add_fusion.4, f32[128,1024]{1,0:T(8,128)S(1)} %convert_add_fusion.5), kind=kOutput, calls=%fused_computation.19 | convolution fusion | flops 1882062848 | bytes 17695232 | tf_op jit(solution)/shard_map/dot_general | solution.py:91
  89.4 0.2 reduce-scatter.5.cloned.1.call-start
  89.7 0.1 convert_add_fusion.1
  89.8 4.1 %collective-permute-done.5 = bf16[128,1024]{1,0:T(8,128)(2,1)S(1)} collective-permute-done((bf16[128,1024]{1,0:T(8,128)(2,1)S(1)}, bf16[128,1024]{1,0:T(8,128)(2,1)S(1)}, u32[]{:S(2)}, u32[]{:S(2)}) %collective-permute-start.5) | collective-permute-done | bytes 262176 | tf_op jit(solution)/shard_map/ppermute | solution.py:14
  93.9 1.8 multiply_convert_fusion.2
  95.7 15.5 %convolution_convert_fusion.1 = bf16[128,3584]{1,0:T(8,128)(2,1)} fusion(bf16[128,2048]{1,0:T(8,128)(2,1)S(1)} %get-tuple-element.4, bf16[128,2048]{1,0:T(8,128)(2,1)S(1)} %get-tuple-element.3, bf16[1,3584,4096]{2,1,0:T(8,128)(2,1)} %param.10), kind=kOutput, calls=%fused_computation.20 | convolution fusion | flops 3760652288 | bytes 31326208 | tf_op jit(solution)/shard_map/dot_general | solution.py:95
  111.2 14.4 %fusion = bf16[1,3584,4096]{2,1,0:T(8,128)(2,1)} fusion(bf16[128,2048]{1,0:T(8,128)(2,1)S(1)} %get-tuple-element.4, bf16[128,2048]{1,0:T(8,128)(2,1)S(1)} %get-tuple-element.3, bf16[128,3712]{1,0:T(8,128)(2,1)S(1)} %all_gather.6, pred[128]{0:T(512)(128)(4,1)S(1)} %broadcast_compare_fusion), kind=kOutput, calls=%fused_computation.1 | convolution fusion | flops 3775332352 | bytes 31326720 | tf_op jit(solution)/shard_map/dot_general | solution.py:99
  125.6 19.0 %reduce-scatter.3.cloned.1.call-done = bf16[8,3584]{1,0:T(8,128)(2,1)} async-done(((bf16[128,3584]{1,0:T(8,128)(2,1)}), bf16[8,3584]{1,0:T(8,128)(2,1)}) %reduce-scatter.3.cloned.1.call-update) | async-done | bytes 57360 | tf_op jit(solution)/shard_map/reduce_scatter | solution.py:94
  144.6 60.7 %reduce-scatter.5.cloned.1.call-done = bf16[8,3584]{1,0:T(8,128)(2,1)} async-done(((bf16[128,3584]{1,0:T(8,128)(2,1)}), bf16[8,3584]{1,0:T(8,128)(2,1)}) %reduce-scatter.5.cloned.1.call-update) | async-done | bytes 57360 | tf_op jit(solution)/shard_map/reduce_scatter | solution.py:98
  (27 shorter events, 0.3 us)
Async XLA Ops:
  7.2 137.5 %reduce-scatter.3.cloned.1.call-start = ((), (), s32[]{:S(2)}) async-start(), calls=%async_computation.2 | async-start | bytes 974848 | tf_op jit(solution)/shard_map/reduce_scatter | solution.py:94
  39.3 44.1 %collective-permute-start = (bf16[128,1024]{1,0:T(8,128)(2,1)S(1)}, bf16[128,1024]{1,0:T(8,128)(2,1)S(1)}, u32[]{:S(2)}, u32[]{:S(2)}) collective-permute-start(bf16[128,1024]{1,0:T(8,128)(2,1)S(1)} %fusion.29), channel_id=1, source_target_pairs={{0,1},{1,0},{2,3},{3,2},{4,5},{5,4},{6,7},{7,6},{8,9},{9,8},{10,11... | collective-permute-start | bytes 786440 | tf_op jit(solution)/shard_map/ppermute | solution.py:14
  40.8 36.2 %slice-start = ((s8[14680064]{0:T(1024)(128)(4,1)}), s8[4194304]{0:T(1024)(128)(4,1)S(1)}, s32[]{:S(2)}) async-start(s8[14680064]{0:T(1024)(128)(4,1)} %bitcast.26), calls=%async_computation.4 | async-start | bytes 8388608
  40.8 36.2 %slice-start.1 = ((s8[14680064]{0:T(1024)(128)(4,1)}), s8[4194304]{0:T(1024)(128)(4,1)S(1)}, s32[]{:S(2)}) async-start(s8[14680064]{0:T(1024)(128)(4,1)} %bitcast.26), calls=%async_computation.5 | async-start | bytes 8388608
  45.2 31.8 %slice-start.2 = ((s8[14680064]{0:T(1024)(128)(4,1)}), s8[4194304]{0:T(1024)(128)(4,1)S(1)}, s32[]{:S(2)}) async-start(s8[14680064]{0:T(1024)(128)(4,1)} %bitcast.26), calls=%async_computation.6 | async-start | bytes 8388608
  45.3 39.1 %collective-permute-start.3 = (bf16[128,1024]{1,0:T(8,128)(2,1)S(1)}, bf16[128,1024]{1,0:T(8,128)(2,1)S(1)}, u32[]{:S(2)}, u32[]{:S(2)}) collective-permute-start(bf16[128,1024]{1,0:T(8,128)(2,1)S(1)} %fusion.38), channel_id=1, source_target_pairs={{0,1},{1,0},{2,3},{3,2},{4,5},{5,4},{6,7},{7,6},{8,9},{9,8},{10,11... | collective-permute-start | bytes 786440 | tf_op jit(solution)/shard_map/ppermute | solution.py:14
  50.5 6.4 %copy-start.2 = (bf16[8,3584]{1,0:T(8,128)(2,1)S(1)}, bf16[8,3584]{1,0:T(8,128)(2,1)}, u32[]{:S(2)}) copy-start(bf16[8,3584]{1,0:T(8,128)(2,1)} %param.7) | copy-start | bytes 172036
  50.5 26.5 %slice-start.3 = ((s8[14680064]{0:T(1024)(128)(4,1)}), s8[2097152]{0:T(1024)(128)(4,1)S(1)}, s32[]{:S(2)}) async-start(s8[14680064]{0:T(1024)(128)(4,1)} %bitcast.26), calls=%async_computation.7 | async-start | bytes 4194304
  50.6 33.9 %collective-permute-start.2 = (bf16[128,1024]{1,0:T(8,128)(2,1)S(1)}, bf16[128,1024]{1,0:T(8,128)(2,1)S(1)}, u32[]{:S(2)}, u32[]{:S(2)}) collective-permute-start(bf16[128,1024]{1,0:T(8,128)(2,1)S(1)} %fusion.35), channel_id=1, source_target_pairs={{0,1},{1,0},{2,3},{3,2},{4,5},{5,4},{6,7},{7,6},{8,9},{9,8},{10,11... | collective-permute-start | bytes 786440 | tf_op jit(solution)/shard_map/ppermute | solution.py:14
  55.9 28.6 %collective-permute-start.1 = (bf16[128,1024]{1,0:T(8,128)(2,1)S(1)}, bf16[128,1024]{1,0:T(8,128)(2,1)S(1)}, u32[]{:S(2)}, u32[]{:S(2)}) collective-permute-start(bf16[128,1024]{1,0:T(8,128)(2,1)S(1)} %fusion.32), channel_id=1, source_target_pairs={{0,1},{1,0},{2,3},{3,2},{4,5},{5,4},{6,7},{7,6},{8,9},{9,8},{10,11... | collective-permute-start | bytes 786440 | tf_op jit(solution)/shard_map/ppermute | solution.py:14
  79.6 10.1 %collective-permute-start.4 = (bf16[128,1024]{1,0:T(8,128)(2,1)S(1)}, bf16[128,1024]{1,0:T(8,128)(2,1)S(1)}, u32[]{:S(2)}, u32[]{:S(2)}) collective-permute-start(bf16[128,1024]{1,0:T(8,128)(2,1)S(1)} %fusion.23), channel_id=1, source_target_pairs={{0,1},{1,0},{2,3},{3,2},{4,5},{5,4},{6,7},{7,6},{8,9},{9,8},{10,11... | collective-permute-start | bytes 786440 | tf_op jit(solution)/shard_map/ppermute | solution.py:14
  83.4 10.5 %collective-permute-start.5 = (bf16[128,1024]{1,0:T(8,128)(2,1)S(1)}, bf16[128,1024]{1,0:T(8,128)(2,1)S(1)}, u32[]{:S(2)}, u32[]{:S(2)}) collective-permute-start(bf16[128,1024]{1,0:T(8,128)(2,1)S(1)} %fusion.26), channel_id=1, source_target_pairs={{0,1},{1,0},{2,3},{3,2},{4,5},{5,4},{6,7},{7,6},{8,9},{9,8},{10,11... | collective-permute-start | bytes 786440 | tf_op jit(solution)/shard_map/ppermute | solution.py:14
  84.5 0.8 copy-start
  85.3 0.8 copy-start.1
  89.4 115.9 %reduce-scatter.5.cloned.1.call-start = ((), (), s32[]{:S(2)}) async-start(), calls=%async_computation.3 | async-start | bytes 974848 | tf_op jit(solution)/shard_map/reduce_scatter | solution.py:98
Sparse Core Ops, SparseCore 0:
  89.6 55.0 reduce-scatter.2
  149.2 56.0 reduce-scatter.4

commit v2 on v1

--- a/solution.py
+++ b/solution.py
@@ -1,6 +1,8 @@
 import jax
 import jax.numpy as jnp
 from jax import lax
+from jax.experimental import pallas as pl
+from jax.experimental.pallas import tpu as pltpu
 from jax.sharding import PartitionSpec as P
 
 FF = 2048
@@ -13,6 +15,84 @@
         return lax.psum(sent, "dp").astype(jnp.float32)
     other = lax.ppermute(sent, "dp", [(0, 1), (1, 0)])
     return sent.astype(jnp.float32) + other.astype(jnp.float32)
+
+
+def from_partner(block, offset, ep_count):
+    return lax.ppermute(block, "ep", [(i, i ^ offset) for i in range(ep_count)])
+
+
+def far_offsets(ep_count):
+    return range(4, ep_count, 4)
+
+
+def gather_far(block, ep_count):
+    return jnp.concatenate(
+        [block] + [from_partner(block, offset, ep_count) for offset in far_offsets(ep_count)]
+    )
+
+
+def gather_near(rows, ep_count):
+    for offset in (2, 1):
+        rows = jnp.concatenate([rows, from_partner(rows, offset, ep_count)])
+    return rows
+
+
+def sum_near(kept, offset, ep_count, beside):
+    half = kept.shape[0] // 2
+    sent, beside = lax.optimization_barrier((kept[half:].astype(jnp.bfloat16), beside))
+    other = from_partner(sent, offset, ep_count)
+    return (lambda: kept[:half].astype(jnp.float32) + other.astype(jnp.float32)), beside
+
+
+def sum_far(kept, ep_count, beside):
+    size = kept.shape[0] // (ep_count // 4)
+    sent, beside = lax.optimization_barrier((kept.astype(jnp.bfloat16), beside))
+    others = [
+        from_partner(sent[number * size : (number + 1) * size], offset, ep_count)
+        for number, offset in enumerate(far_offsets(ep_count), 1)
+    ]
+
+    def finish():
+        total = kept[:size]
+        for other in others:
+            total = total + other.astype(jnp.float32)
+        return total.astype(jnp.bfloat16)
+
+    return finish, beside
+
+
+def grad_kernel(x_ref, g_ref, *refs):
+    o_ref = refs[-1]
+    columns = o_ref.shape[1]
+    step = min(1024, columns)
+    for at in range(0, columns, step):
+        o_ref[:, at : at + step] = jnp.dot(
+            x_ref[...], g_ref[:, at : at + step], preferred_element_type=jnp.float32
+        ).astype(o_ref.dtype)
+
+
+def grad_part(x_turned, pair, start, count, block, whole):
+    width, rows = x_turned.shape
+    columns = pair.shape[1]
+    given = () if whole is None else (whole,)
+    return pl.pallas_call(
+        grad_kernel,
+        out_shape=jax.ShapeDtypeStruct((width, columns), jnp.bfloat16),
+        grid=(count,),
+        in_specs=[
+            pl.BlockSpec((block, rows), lambda i: (i + start, 0)),
+            pl.BlockSpec((rows, columns), lambda i: (0, 0)),
+        ]
+        + [pl.BlockSpec(memory_space=pl.ANY)] * len(given),
+        out_specs=pl.BlockSpec((block, columns), lambda i: (i + start, 0)),
+        input_output_aliases={2: 0} if given else {},
+        cost_estimate=pl.CostEstimate(
+            flops=2 * count * block * rows * columns,
+            bytes_accessed=2 * count * block * (columns + rows) + 2 * rows * columns,
+            transcendentals=0,
+        ),
+        compiler_params=pltpu.CompilerParams(vmem_limit_bytes=32 * 2**20),
+    )(x_turned, pair, *given)
 
 
 def on_device(tokens, cotangent, routes, route_weights, gate_up, down_proj):
@@ -37,8 +117,10 @@
     low = rest - middle
     packed = jnp.concatenate([high, middle, low], axis=1).astype(jnp.bfloat16)
     packed = jnp.pad(packed, ((0, 0), (0, -packed.shape[1] % 128)))
-    first = lax.all_gather(jnp.concatenate([tokens, packed], axis=1), "ep", axis=0, tiled=True)
-    d_all = lax.all_gather(cotangent, "ep", axis=0, tiled=True)
+    first = gather_far(jnp.concatenate([tokens, packed], axis=1), ep_count)
+    first, cotangent = lax.optimization_barrier((first, cotangent))
+    first = gather_near(first, ep_count)
+    d_far = gather_far(cotangent, ep_count)
     x_all = first[:, :width]
     parts = first[:, width:].astype(jnp.float32)
     mine = jnp.arange(experts, dtype=jnp.int32)[None, :] == expert
@@ -54,17 +136,25 @@
     )
     named = weight > 0.0
     x_rows = jnp.where(named, x_all, jnp.zeros_like(x_all))
-    d_rows = (weight * d_all.astype(jnp.float32)).astype(jnp.bfloat16)
     w_pair = gate_up[0]
     w_down = down_proj[0]
     piece = min(PIECE, hidden_units)
-    pre = [
-        dp_sum(
-            jnp.dot(x_rows, w_pair[:, at : at + piece], preferred_element_type=jnp.float32),
-            dp_count,
-        )
-        for at in range(0, 2 * hidden_units, piece)
-    ]
+    starts = list(range(0, 2 * hidden_units, piece))
+    d_far, x_rows = lax.optimization_barrier((d_far, x_rows))
+    d_near = jnp.concatenate([d_far, from_partner(d_far, 2, ep_count)])
+
+    def pre_piece(at, x):
+        return jnp.dot(
+            x, w_pair[:, at : at + piece], preferred_element_type=jnp.float32
+        ).astype(jnp.bfloat16)
+
+    early = len(starts) // 2
+    terms = [pre_piece(at, x_rows) for at in starts[:early]]
+    d_near, x_late = lax.optimization_barrier((d_near, x_rows))
+    d_all = jnp.concatenate([d_near, from_partner(d_near, 1, ep_count)])
+    terms += [pre_piece(at, x_late) for at in starts[early:]]
+    pre = [dp_sum(term, dp_count) for term in terms]
+    d_rows = (weight * d_all.astype(jnp.float32)).astype(jnp.bfloat16)
     back = [
         dp_sum(
             lax.dot_general(
@@ -91,14 +181,43 @@
     out_rows = (weight * jnp.dot(hidden, w_down, preferred_element_type=jnp.float32)).astype(
         jnp.bfloat16
     )
-    mixed = lax.psum_scatter(out_rows, "ep", scatter_dimension=0, tiled=True)
-    dx_rows = lax.dot_general(
-        grad_pair, w_pair, (((1,), (1,)), ((), ())), preferred_element_type=jnp.float32
-    ).astype(jnp.bfloat16)
-    token_grad = lax.psum_scatter(dx_rows, "ep", scatter_dimension=0, tiled=True)
-    weight_grad = lax.dot_general(
-        x_rows, grad_pair, (((0,), (0,)), ((), ())), preferred_element_type=jnp.float32
-    ).astype(jnp.bfloat16)
+    strip = width // 4 if width % 512 == 0 else width // 2
+
+    def dx_strips(pair, begin, end):
+        return [
+            lax.dot_general(
+                pair,
+                w_pair[at : at + strip],
+                (((1,), (1,)), ((), ())),
+                preferred_element_type=jnp.float32,
+            ).astype(jnp.bfloat16)
+            for at in range(begin, end, strip)
+        ]
+
+    finish, pair = sum_near(out_rows, 1, ep_count, grad_pair)
+    strips = dx_strips(pair, 0, strip)
+    finish, pair = sum_near(finish(), 2, ep_count, pair)
+    strips += dx_strips(pair, strip, width // 2)
+    finish, pair = sum_far(finish(), ep_count, pair)
+    strips += dx_strips(pair, width // 2, width)
+    mixed = finish()
+    dx_rows = jnp.concatenate(strips, axis=1)
+    block = 256 if width % 256 == 0 else width
+    blocks = width // block
+    cuts = (0, blocks // 4, blocks * 9 // 16, blocks)
+    x_turned = x_rows.T
+    whole = None
+    finish, x_turned = sum_near(dx_rows, 1, ep_count, x_turned)
+    for number in range(3):
+        count = cuts[number + 1] - cuts[number]
+        if count > 0:
+            whole = grad_part(x_turned, grad_pair, cuts[number], count, block, whole)
+        if number == 0:
+            finish, x_turned = sum_near(finish(), 2, ep_count, x_turned)
+        if number == 1:
+            finish, x_turned = sum_far(finish(), ep_count, x_turned)
+    token_grad = finish()
+    weight_grad = whole
     return (mixed, token_grad, weight_grad[None])
 
 

time: 213 us -> 130 us (0.61)
  waiting for transfers between devices: 83.8 us -> 28.6 us
  blocking collectives: 45.9 us -> 0 us
  starting transfers between devices: 6.75 us -> 26.3 us
  Pallas kernels: 0 us -> 16.8 us
  between operations: 14.3 us -> 1.03 us
  matrix products: 55.8 us -> 46.9 us
  other arithmetic: 4.04 us -> 8.36 us
    reduce_scatter x2 -> x0, waiting for transfers between devices: 79.7 us -> none  [the longest x1 60.7 us: on_device(): lax.psum_scatter(dx_rows, 'ep', scatter_dimension=0, tiled=True)]
    all_gather x2 -> x0, blocking collectives: 45.9 us -> none  [the longest x1 25.9 us: on_device(): lax.all_gather(jnp.concatenate([tokens, packed], axis=1), 'ep', axis=0, t...]
    ppermute x0 -> x20, starting transfers between devices: none -> 20 us  [from_partner(): return lax.ppermute(block, 'ep', [(i, i ^ offset) for i in range(ep_count)])]
    pallas_call x0 -> x3, Pallas kernels: none -> 16.8 us  [grad_part(): pl.pallas_call(grad_kernel, out_shape=jax.ShapeDtypeStruct((width, column...]
    ppermute x6, waiting for transfers between devices: 4.1 us -> 17.7 us  [dp_sum(): other = lax.ppermute(sent, 'dp', [(0, 1), (1, 0)])]
    ppermute x0 -> x20, waiting for transfers between devices: none -> 10.9 us  [from_partner(): return lax.ppermute(block, 'ep', [(i, i ^ offset) for i in range(ep_count)])]
    dot_general x6 -> x8, matrix products: 47.5 us -> 39.4 us  [the longest x4 22.1 us: dx_strips(): lax.dot_general(pair, w_pair[at:at + strip], (((1,), (1,)), ((), ())), pr...]
  transfers between devices with their start and end apart: 8 -> 26, of which waited for: 3 -> 13; matrix products, arithmetic and copies ran while one was open for 25% -> 28% of each run, Pallas kernels for 0% -> 13%
where the time goes in v2:
time: 130 us
  matrix products  46.9 us (36%)
  waiting for transfers between devices  28.6 us (22%)
  starting transfers between devices  26.3 us (20%)
  Pallas kernels  16.8 us (13%)
  other arithmetic  8.36 us (6%)
  local copies, waits for them, and re-layouts  1.53 us (1%)
    dot_general x4, matrix products, dx_strips(): lax.dot_general(pair, w_pair[at:at + strip], (((1,), (1,)), ((), ())), pr...  22.1 us
    ppermute x20, starting transfers between devices, from_partner(): return lax.ppermute(block, 'ep', [(i, i ^ offset) for i in range(ep_count)])  20 us
    ppermute x6, waiting for transfers between devices, dp_sum(): other = lax.ppermute(sent, 'dp', [(0, 1), (1, 0)])  17.7 us
    dot_general x4, matrix products, pre_piece(): jnp.dot(x, w_pair[:, at:at + piece], preferred_element_type=jnp.float32)  17.4 us
    pallas_call x3, Pallas kernels, grad_part(): pl.pallas_call(grad_kernel, out_shape=jax.ShapeDtypeStruct((width, column...  16.8 us
    ppermute x20, waiting for transfers between devices, from_partner(): return lax.ppermute(block, 'ep', [(i, i ^ offset) for i in range(ep_count)])  10.9 us
    ppermute x6, starting transfers between devices, dp_sum(): other = lax.ppermute(sent, 'dp', [(0, 1), (1, 0)])  6.33 us
    dot_general x2, matrix products, on_device(): lax.dot_general(d_rows, w_down[at:at + piece], (((1,), (1,)), ((), ())),...  5.02 us
  transfers between devices with their start and end apart: 26, of which 13 were waited for; matrix products, arithmetic and copies ran while one was open for 28% of the time, Pallas kernels for 13%

profile of v2, /device:TPU:0, one launch (start us, length us, event | category | flops | bytes accessed | tf_op | source)
XLA Modules:
  0.0 129.5 jit_solution(2141413994591292092)
XLA Ops:
  2.3 5.0 %collective-permute-start.2 = (bf16[8,3712]{1,0:T(8,128)(2,1)S(1)}, bf16[8,3712]{1,0:T(8,128)(2,1)S(1)}, u32[]{:S(2)}, u32[]{:S(2)}) collective-permute-start(bf16[8,3712]{1,0:T(8,128)(2,1)S(1)} %pad_maximum_fusion.11), channel_id=1, source_target_pairs={{0,24},{2,26},{4,28},{6,30},{8,16},{10,18},{12,20},{14,22},{16,8},... | collective-permute-start | bytes 178184 | tf_op jit(solution)/shard_map/ppermute | solution.py:21
  8.0 1.9 %collective-permute-done.2 = bf16[8,3712]{1,0:T(8,128)(2,1)S(1)} collective-permute-done((bf16[8,3712]{1,0:T(8,128)(2,1)S(1)}, bf16[8,3712]{1,0:T(8,128)(2,1)S(1)}, u32[]{:S(2)}, u32[]{:S(2)}) %collective-permute-start.2) | collective-permute-done | bytes 59424 | tf_op jit(solution)/shard_map/ppermute | solution.py:21
  9.8 2.7 %collective-permute-done.1 = bf16[8,3712]{1,0:T(8,128)(2,1)S(1)} collective-permute-done((bf16[8,3712]{1,0:T(8,128)(2,1)S(1)}, bf16[8,3712]{1,0:T(8,128)(2,1)S(1)}, u32[]{:S(2)}, u32[]{:S(2)}) %collective-permute-start.1) | collective-permute-done | bytes 59424 | tf_op jit(solution)/shard_map/ppermute | solution.py:21
  13.4 1.7 %collective-permute-start.3 = (bf16[32,3712]{1,0:T(8,128)(2,1)S(1)}, bf16[32,3712]{1,0:T(8,128)(2,1)S(1)}, u32[]{:S(2)}, u32[]{:S(2)}) collective-permute-start(bf16[32,3712]{1,0:T(8,128)(2,1)S(1)} %pad_maximum_fusion.9), channel_id=1, source_target_pairs={{0,4},{2,6},{4,0},{6,2},{8,12},{10,14},{12,8},{14,10},{16,20},{18,... | collective-permute-start | bytes 712712 | tf_op jit(solution)/shard_map/ppermute | solution.py:21
  15.1 2.5 %collective-permute-start.7 = (bf16[8,3584]{1,0:T(8,128)(2,1)}, bf16[8,3584]{1,0:T(8,128)(2,1)S(1)}, u32[]{:S(2)}, u32[]{:S(2)}) collective-permute-start(bf16[8,3584]{1,0:T(8,128)(2,1)} %param.7), channel_id=1, source_target_pairs={{0,24},{2,26},{4,28},{6,30},{8,16},{10,18},{12,20},{14,22},{16,8},... | collective-permute-start | bytes 172040 | tf_op jit(solution)/shard_map/ppermute | solution.py:21
  17.6 1.8 %collective-permute-start.5 = (bf16[8,3584]{1,0:T(8,128)(2,1)}, bf16[8,3584]{1,0:T(8,128)(2,1)S(1)}, u32[]{:S(2)}, u32[]{:S(2)}) collective-permute-start(bf16[8,3584]{1,0:T(8,128)(2,1)} %param.7), channel_id=1, source_target_pairs={{0,8},{2,10},{4,12},{6,14},{8,0},{10,2},{12,4},{14,6},{16,24},{18,... | collective-permute-start | bytes 172040 | tf_op jit(solution)/shard_map/ppermute | solution.py:21
  26.9 4.2 %fusion.43 = bf16[128,1024]{1,0:T(8,128)(2,1)S(1)} fusion(bf16[128,3584]{0,1:T(8,128)(2,1)S(1)} %fusion.65, bf16[3584,4096]{1,0:T(8,128)(2,1)} %bitcast.52), kind=kOutput, calls=%fused_computation.34 | convolution fusion | flops 939655168 | bytes 8519680 | tf_op jit(solution)/shard_map/dot_general | solution.py:147
  31.2 4.4 %fusion.40 = bf16[128,1024]{1,0:T(8,128)(2,1)S(1)} fusion(bf16[128,3584]{0,1:T(8,128)(2,1)S(1)} %fusion.65, bf16[3584,4096]{1,0:T(8,128)(2,1)} %bitcast.53), kind=kOutput, calls=%fused_computation.33 | convolution fusion | flops 939655168 | bytes 8519680 | tf_op jit(solution)/shard_map/dot_general | solution.py:147
  35.5 1.5 %collective-permute-start.8 = (bf16[128,1024]{1,0:T(8,128)(2,1)S(1)}, bf16[128,1024]{1,0:T(8,128)(2,1)S(1)}, u32[]{:S(2)}, u32[]{:S(2)}) collective-permute-start(bf16[128,1024]{1,0:T(8,128)(2,1)S(1)} %fusion.40), channel_id=1, source_target_pairs={{0,1},{1,0},{2,3},{3,2},{4,5},{5,4},{6,7},{7,6},{8,9},{9,8},{10,11... | collective-permute-start | bytes 786440 | tf_op jit(solution)/shard_map/ppermute | solution.py:16
  37.7 4.4 %fusion.49 = bf16[128,1024]{1,0:T(8,128)(2,1)S(1)} fusion(bf16[128,3584]{0,1:T(8,128)(2,1)S(1)} %fusion.65, bf16[3584,4096]{1,0:T(8,128)(2,1)} %bitcast.54), kind=kOutput, calls=%fused_computation.36 | convolution fusion | flops 939655168 | bytes 8519680 | tf_op jit(solution)/shard_map/dot_general | solution.py:147
  42.1 4.4 %fusion.46 = bf16[128,1024]{1,0:T(8,128)(2,1)S(1)} fusion(bf16[128,3584]{0,1:T(8,128)(2,1)S(1)} %fusion.65, bf16[3584,4096]{1,0:T(8,128)(2,1)} %bitcast.55), kind=kOutput, calls=%fused_computation.35 | convolution fusion | flops 939655168 | bytes 8519680 | tf_op jit(solution)/shard_map/dot_general | solution.py:147
  46.5 1.6 %collective-permute-start.11 = (bf16[128,1024]{1,0:T(8,128)(2,1)S(1)}, bf16[128,1024]{1,0:T(8,128)(2,1)S(1)}, u32[]{:S(2)}, u32[]{:S(2)}) collective-permute-start(bf16[128,1024]{1,0:T(8,128)(2,1)S(1)} %fusion.46), channel_id=1, source_target_pairs={{0,1},{1,0},{2,3},{3,2},{4,5},{5,4},{6,7},{7,6},{8,9},{9,8},{10,11... | collective-permute-start | bytes 786440 | tf_op jit(solution)/shard_map/ppermute | solution.py:16
  48.6 1.4 %collective-permute-done.9 = bf16[128,1024]{1,0:T(8,128)(2,1)S(1)} collective-permute-done((bf16[128,1024]{1,0:T(8,128)(2,1)S(1)}, bf16[128,1024]{1,0:T(8,128)(2,1)S(1)}, u32[]{:S(2)}, u32[]{:S(2)}) %collective-permute-start.9) | collective-permute-done | bytes 262176 | tf_op jit(solution)/shard_map/ppermute | solution.py:16
  50.2 5.6 %collective-permute-done.11 = bf16[128,1024]{1,0:T(8,128)(2,1)S(1)} collective-permute-done((bf16[128,1024]{1,0:T(8,128)(2,1)S(1)}, bf16[128,1024]{1,0:T(8,128)(2,1)S(1)}, u32[]{:S(2)}, u32[]{:S(2)}) %collective-permute-start.11) | collective-permute-done | bytes 262176 | tf_op jit(solution)/shard_map/ppermute | solution.py:16
  55.9 4.7 %collective-permute-done.12 = bf16[128,1024]{1,0:T(8,128)(2,1)S(1)} collective-permute-done((bf16[128,1024]{1,0:T(8,128)(2,1)S(1)}, bf16[128,1024]{1,0:T(8,128)(2,1)S(1)}, u32[]{:S(2)}, u32[]{:S(2)}) %collective-permute-start.12) | collective-permute-done | bytes 262176 | tf_op jit(solution)/shard_map/ppermute | solution.py:16
  60.7 2.5 %fusion.34 = bf16[128,1024]{1,0:T(8,128)(2,1)S(1)} fusion(bf16[1,2048,3584]{2,1,0:T(8,128)(2,1)S(1)} %bitcast.57, bf16[64,3584]{1,0:T(8,128)(2,1)S(1)} %collective-permute-done.13, bf16[64,3584]{1,0:T(8,128)(2,1)S(1)} %pad_maximum_fusion.8, f32[128]{0:T(128)S(1)} %fusion.74), kind=kOutput, calls=%fused_computation.31 | convolution fusion | flops 942407680 | bytes 8520192 | tf_op jit(solution)/shard_map/dot_general | solution.py:160
  63.2 1.6 %collective-permute-start.14 = (bf16[128,1024]{1,0:T(8,128)(2,1)S(1)}, bf16[128,1024]{1,0:T(8,128)(2,1)S(1)}, u32[]{:S(2)}, u32[]{:S(2)}) collective-permute-start(bf16[128,1024]{1,0:T(8,128)(2,1)S(1)} %fusion.34), channel_id=1, source_target_pairs={{0,1},{1,0},{2,3},{3,2},{4,5},{5,4},{6,7},{7,6},{8,9},{9,8},{10,11... | collective-permute-start | bytes 786440 | tf_op jit(solution)/shard_map/ppermute | solution.py:16
  64.7 2.5 %fusion.37 = bf16[128,1024]{1,0:T(8,128)(2,1)S(1)} fusion(bf16[1,2048,3584]{2,1,0:T(8,128)(2,1)S(1)} %bitcast.57, bf16[64,3584]{1,0:T(8,128)(2,1)S(1)} %collective-permute-done.13, bf16[64,3584]{1,0:T(8,128)(2,1)S(1)} %pad_maximum_fusion.8, f32[128]{0:T(128)S(1)} %fusion.74), kind=kOutput, calls=%fused_computation.32 | convolution fusion | flops 942407680 | bytes 8520192 | tf_op jit(solution)/shard_map/dot_general | solution.py:160
  67.8 2.4 %fusion.31 = bf16[128,3584]{1,0:T(8,128)(2,1)S(1)} fusion(bf16[1,2048,3584]{2,1,0:T(8,128)(2,1)S(1)} %bitcast.57, f32[128]{0:T(128)S(1)} %fusion.74, f32[128,1024]{1,0:T(8,128)S(1)} %convert_add_fusion.4, f32[128,1024]{1,0:T(8,128)S(1)} %convert_add_fusion.5, f32[128,1024]{1,0:T(8,128)S(1)} %convert_add_fusion.6, f32[128,1024]{1,0:T(8,128)S(1)} %convert_add_fusion.7), kind=kOutput, calls=%fused_computation.29 | convolution fusion | flops 1882062848 | bytes 17695232 | tf_op jit(solution)/shard_map/dot_general | solution.py:181
  70.3 2.2 %collective-permute-done.14 = bf16[128,1024]{1,0:T(8,128)(2,1)S(1)} collective-permute-done((bf16[128,1024]{1,0:T(8,128)(2,1)S(1)}, bf16[128,1024]{1,0:T(8,128)(2,1)S(1)}, u32[]{:S(2)}, u32[]{:S(2)}) %collective-permute-start.14) | collective-permute-done | bytes 262176 | tf_op jit(solution)/shard_map/ppermute | solution.py:16
  72.5 3.8 %collective-permute-done.15 = bf16[128,1024]{1,0:T(8,128)(2,1)S(1)} collective-permute-done((bf16[128,1024]{1,0:T(8,128)(2,1)S(1)}, bf16[128,1024]{1,0:T(8,128)(2,1)S(1)}, u32[]{:S(2)}, u32[]{:S(2)}) %collective-permute-start.15) | collective-permute-done | bytes 262176 | tf_op jit(solution)/shard_map/ppermute | solution.py:16
  77.1 5.5 %fusion.52 = bf16[128,896]{1,0:T(8,128)(2,1)S(1)} fusion(bf16[128,4096]{1,0:T(8,128)(2,1)S(1)} %pad_maximum_fusion.3.g_ref, bf16[1,3584,4096]{2,1,0:T(8,128)(2,1)} %param.10), kind=kOutput, calls=%fused_computation.37 | convolution fusion | flops 939638784 | bytes 8617984 | tf_op jit(solution)/shard_map/dot_general | solution.py:188
  82.9 5.5 %fusion.55 = bf16[128,896]{1,0:T(8,128)(2,1)S(1)} fusion(bf16[128,4096]{1,0:T(8,128)(2,1)S(1)} %pad_maximum_fusion.3.g_ref, bf16[1,3584,4096]{2,1,0:T(8,128)(2,1)} %param.10), kind=kOutput, calls=%fused_computation.38 | convolution fusion | flops 939638784 | bytes 8617984 | tf_op jit(solution)/shard_map/dot_general | solution.py:188
  88.5 2.5 %collective-permute-done.17 = bf16[32,3584]{1,0:T(8,128)(2,1)S(1)} collective-permute-done((bf16[32,3584]{1,0:T(8,128)(2,1)S(1)}, bf16[32,3584]{1,0:T(8,128)(2,1)S(1)}, u32[]{:S(2)}, u32[]{:S(2)}) %collective-permute-start.17) | collective-permute-done | bytes 229408 | tf_op jit(solution)/shard_map/ppermute | solution.py:21
  91.0 5.5 %fusion.61 = bf16[128,896]{1,0:T(8,128)(2,1)S(1)} fusion(bf16[128,4096]{1,0:T(8,128)(2,1)S(1)} %pad_maximum_fusion.3.g_ref, bf16[1,3584,4096]{2,1,0:T(8,128)(2,1)} %param.10), kind=kOutput, calls=%fused_computation.40 | convolution fusion | flops 939638784 | bytes 8617984 | tf_op jit(solution)/shard_map/dot_general | solution.py:188
  96.5 5.5 %fusion.58 = bf16[128,896]{1,0:T(8,128)(2,1)S(1)} fusion(bf16[128,4096]{1,0:T(8,128)(2,1)S(1)} %pad_maximum_fusion.3.g_ref, bf16[1,3584,4096]{2,1,0:T(8,128)(2,1)} %param.10), kind=kOutput, calls=%fused_computation.39 | convolution fusion | flops 939638784 | bytes 8617984 | tf_op jit(solution)/shard_map/dot_general | solution.py:188
  102.6 1.4 %collective-permute-start.20 = (bf16[8,3584]{1,0:T(8,128)(2,1)S(1)}, bf16[8,3584]{1,0:T(8,128)(2,1)S(1)}, u32[]{:S(2)}, u32[]{:S(2)}) collective-permute-start(bf16[8,3584]{1,0:T(8,128)(2,1)S(1)} %get-tuple-element.49), channel_id=1, source_target_pairs={{0,24},{2,26},{4,28},{6,30},{8,16},{10,18},{12,20},{14,22},{16,8},... | collective-permute-start | bytes 172040 | tf_op jit(solution)/shard_map/ppermute | solution.py:21
  104.0 1.8 %collective-permute-start.19 = (bf16[8,3584]{1,0:T(8,128)(2,1)S(1)}, bf16[8,3584]{1,0:T(8,128)(2,1)S(1)}, u32[]{:S(2)}, u32[]{:S(2)}) collective-permute-start(bf16[8,3584]{1,0:T(8,128)(2,1)S(1)} %get-tuple-element.50), channel_id=1, source_target_pairs={{0,16},{2,18},{4,20},{6,22},{8,24},{10,26},{12,28},{14,30},{16,0},... | collective-permute-start | bytes 172040 | tf_op jit(solution)/shard_map/ppermute | solution.py:21
  105.8 4.0 %shard_map.85.refs_0_ = bf16[3584,4096]{1,0:T(8,128)(2,1)} custom-call(bf16[3584,128]{1,0:T(8,128)(2,1)S(1)} %bitcast.48, bf16[128,4096]{1,0:T(8,128)(2,1)S(1)} %pad_maximum_fusion.3.g_ref), custom_call_target="tpu_custom_call" | custom-call | flops 805306368 | bytes 7536640 | tf_op jit(solution)/shard_map/pallas_call | solution.py:78
  112.2 4.7 %shard_map.86.refs_0_ = bf16[3584,4096]{1,0:T(8,128)(2,1)} custom-call(bf16[3584,128]{1,0:T(8,128)(2,1)S(1)} %bitcast.49, bf16[128,4096]{1,0:T(8,128)(2,1)S(1)} %pad_maximum_fusion.3.g_ref, bf16[3584,4096]{1,0:T(8,128)(2,1)} %shard_map.85.refs_0_), custom_call_target="tpu_custom_call", output_to_operand_aliasing={{}: (2, {})} | custom-call | flops 1073741824 | bytes 9699328 | tf_op jit(solution)/shard_map/pallas_call | solution.py:78
  118.6 1.5 %collective-permute-start.25 = (bf16[8,3584]{1,0:T(8,128)(2,1)S(1)}, bf16[8,3584]{1,0:T(8,128)(2,1)S(1)}, u32[]{:S(2)}, u32[]{:S(2)}) collective-permute-start(bf16[8,3584]{1,0:T(8,128)(2,1)S(1)} %get-tuple-element.46), channel_id=1, source_target_pairs={{0,24},{2,26},{4,28},{6,30},{8,16},{10,18},{12,20},{14,22},{16,8},... | collective-permute-start | bytes 172040 | tf_op jit(solution)/shard_map/ppermute | solution.py:21
  120.8 8.1 %shard_map.87 = bf16[3584,4096]{1,0:T(8,128)(2,1)} custom-call(bf16[3584,128]{1,0:T(8,128)(2,1)S(1)} %bitcast.50, bf16[128,4096]{1,0:T(8,128)(2,1)S(1)} %pad_maximum_fusion.3.g_ref, bf16[3584,4096]{1,0:T(8,128)(2,1)} %shard_map.86.refs_0_), custom_call_target="tpu_custom_call", output_to_operand_aliasing={{}: (2, {})} | custom-call | flops 1879048192 | bytes 16187392 | tf_op jit(solution)/shard_map/pallas_call | solution.py:78
  (79 shorter events, 19.6 us)
Async XLA Ops:
  2.3 7.5 %collective-permute-start.2 = (bf16[8,3712]{1,0:T(8,128)(2,1)S(1)}, bf16[8,3712]{1,0:T(8,128)(2,1)S(1)}, u32[]{:S(2)}, u32[]{:S(2)}) collective-permute-start(bf16[8,3712]{1,0:T(8,128)(2,1)S(1)} %pad_maximum_fusion.11), channel_id=1, source_target_pairs={{0,24},{2,26},{4,28},{6,30},{8,16},{10,18},{12,20},{14,22},{16,8},... | collective-permute-start | bytes 178184 | tf_op jit(solution)/shard_map/ppermute | solution.py:21
  7.4 5.2 %collective-permute-start.1 = (bf16[8,3712]{1,0:T(8,128)(2,1)S(1)}, bf16[8,3712]{1,0:T(8,128)(2,1)S(1)}, u32[]{:S(2)}, u32[]{:S(2)}) collective-permute-start(bf16[8,3712]{1,0:T(8,128)(2,1)S(1)} %pad_maximum_fusion.11), channel_id=1, source_target_pairs={{0,16},{2,18},{4,20},{6,22},{8,24},{10,26},{12,28},{14,30},{16,0},... | collective-permute-start | bytes 178184 | tf_op jit(solution)/shard_map/ppermute | solution.py:21
  7.4 5.2 %collective-permute-start = (bf16[8,3712]{1,0:T(8,128)(2,1)S(1)}, bf16[8,3712]{1,0:T(8,128)(2,1)S(1)}, u32[]{:S(2)}, u32[]{:S(2)}) collective-permute-start(bf16[8,3712]{1,0:T(8,128)(2,1)S(1)} %pad_maximum_fusion.11), channel_id=1, source_target_pairs={{0,8},{2,10},{4,12},{6,14},{8,0},{10,2},{12,4},{14,6},{16,24},{18,... | collective-permute-start | bytes 178184 | tf_op jit(solution)/shard_map/ppermute | solution.py:21
  13.4 6.9 %collective-permute-start.3 = (bf16[32,3712]{1,0:T(8,128)(2,1)S(1)}, bf16[32,3712]{1,0:T(8,128)(2,1)S(1)}, u32[]{:S(2)}, u32[]{:S(2)}) collective-permute-start(bf16[32,3712]{1,0:T(8,128)(2,1)S(1)} %pad_maximum_fusion.9), channel_id=1, source_target_pairs={{0,4},{2,6},{4,0},{6,2},{8,12},{10,14},{12,8},{14,10},{16,20},{18,... | collective-permute-start | bytes 712712 | tf_op jit(solution)/shard_map/ppermute | solution.py:21
  15.1 6.6 %collective-permute-start.7 = (bf16[8,3584]{1,0:T(8,128)(2,1)}, bf16[8,3584]{1,0:T(8,128)(2,1)S(1)}, u32[]{:S(2)}, u32[]{:S(2)}) collective-permute-start(bf16[8,3584]{1,0:T(8,128)(2,1)} %param.7), channel_id=1, source_target_pairs={{0,24},{2,26},{4,28},{6,30},{8,16},{10,18},{12,20},{14,22},{16,8},... | collective-permute-start | bytes 172040 | tf_op jit(solution)/shard_map/ppermute | solution.py:21
  17.6 5.3 %collective-permute-start.6 = (bf16[8,3584]{1,0:T(8,128)(2,1)}, bf16[8,3584]{1,0:T(8,128)(2,1)S(1)}, u32[]{:S(2)}, u32[]{:S(2)}) collective-permute-start(bf16[8,3584]{1,0:T(8,128)(2,1)} %param.7), channel_id=1, source_target_pairs={{0,16},{2,18},{4,20},{6,22},{8,24},{10,26},{12,28},{14,30},{16,0},... | collective-permute-start | bytes 172040 | tf_op jit(solution)/shard_map/ppermute | solution.py:21
  17.6 5.3 %collective-permute-start.5 = (bf16[8,3584]{1,0:T(8,128)(2,1)}, bf16[8,3584]{1,0:T(8,128)(2,1)S(1)}, u32[]{:S(2)}, u32[]{:S(2)}) collective-permute-start(bf16[8,3584]{1,0:T(8,128)(2,1)} %param.7), channel_id=1, source_target_pairs={{0,8},{2,10},{4,12},{6,14},{8,0},{10,2},{12,4},{14,6},{16,24},{18,... | collective-permute-start | bytes 172040 | tf_op jit(solution)/shard_map/ppermute | solution.py:21
  20.4 3.8 %collective-permute-start.4 = (bf16[64,3712]{1,0:T(8,128)(2,1)S(1)}, bf16[64,3712]{1,0:T(8,128)(2,1)S(1)}, u32[]{:S(2)}, u32[]{:S(2)}) collective-permute-start(bf16[64,3712]{1,0:T(8,128)(2,1)S(1)} %pad_maximum_fusion.7), channel_id=1, source_target_pairs={{0,2},{2,0},{4,6},{6,4},{8,10},{10,8},{12,14},{14,12},{16,18},{18,... | collective-permute-start | bytes 1425416 | tf_op jit(solution)/shard_map/ppermute | solution.py:21
  26.3 11.3 %collective-permute-start.10 = (bf16[32,3584]{1,0:T(8,128)(2,1)S(1)}, bf16[32,3584]{1,0:T(8,128)(2,1)S(1)}, u32[]{:S(2)}, u32[]{:S(2)}) collective-permute-start(bf16[32,3584]{1,0:T(8,128)(2,1)S(1)} %pad_maximum_fusion.10), channel_id=1, source_target_pairs={{0,4},{2,6},{4,0},{6,2},{8,12},{10,14},{12,8},{14,10},{16,20},{18,... | collective-permute-start | bytes 688136 | tf_op jit(solution)/shard_map/ppermute | solution.py:21
  31.1 29.5 %slice-start = ((s8[14680064]{0:T(1024)(128)(4,1)}), s8[4194304]{0:T(1024)(128)(4,1)S(1)}, s32[]{:S(2)}) async-start(s8[14680064]{0:T(1024)(128)(4,1)} %bitcast.56), calls=%async_computation | async-start | bytes 8388608
  31.1 29.5 %slice-start.1 = ((s8[14680064]{0:T(1024)(128)(4,1)}), s8[4194304]{0:T(1024)(128)(4,1)S(1)}, s32[]{:S(2)}) async-start(s8[14680064]{0:T(1024)(128)(4,1)} %bitcast.56), calls=%async_computation.1 | async-start | bytes 8388608
  35.5 13.0 %collective-permute-start.8 = (bf16[128,1024]{1,0:T(8,128)(2,1)S(1)}, bf16[128,1024]{1,0:T(8,128)(2,1)S(1)}, u32[]{:S(2)}, u32[]{:S(2)}) collective-permute-start(bf16[128,1024]{1,0:T(8,128)(2,1)S(1)} %fusion.40), channel_id=1, source_target_pairs={{0,1},{1,0},{2,3},{3,2},{4,5},{5,4},{6,7},{7,6},{8,9},{9,8},{10,11... | collective-permute-start | bytes 786440 | tf_op jit(solution)/shard_map/ppermute | solution.py:16
  37.1 13.0 %collective-permute-start.9 = (bf16[128,1024]{1,0:T(8,128)(2,1)S(1)}, bf16[128,1024]{1,0:T(8,128)(2,1)S(1)}, u32[]{:S(2)}, u32[]{:S(2)}) collective-permute-start(bf16[128,1024]{1,0:T(8,128)(2,1)S(1)} %fusion.43), channel_id=1, source_target_pairs={{0,1},{1,0},{2,3},{3,2},{4,5},{5,4},{6,7},{7,6},{8,9},{9,8},{10,11... | collective-permute-start | bytes 786440 | tf_op jit(solution)/shard_map/ppermute | solution.py:16
  37.7 22.9 %slice-start.2 = ((s8[14680064]{0:T(1024)(128)(4,1)}), s8[4194304]{0:T(1024)(128)(4,1)S(1)}, s32[]{:S(2)}) async-start(s8[14680064]{0:T(1024)(128)(4,1)} %bitcast.56), calls=%async_computation.2 | async-start | bytes 8388608
  42.1 18.6 %slice-start.3 = ((s8[14680064]{0:T(1024)(128)(4,1)}), s8[2097152]{0:T(1024)(128)(4,1)S(1)}, s32[]{:S(2)}) async-start(s8[14680064]{0:T(1024)(128)(4,1)} %bitcast.56), calls=%async_computation.3 | async-start | bytes 4194304
  46.5 9.3 %collective-permute-start.11 = (bf16[128,1024]{1,0:T(8,128)(2,1)S(1)}, bf16[128,1024]{1,0:T(8,128)(2,1)S(1)}, u32[]{:S(2)}, u32[]{:S(2)}) collective-permute-start(bf16[128,1024]{1,0:T(8,128)(2,1)S(1)} %fusion.46), channel_id=1, source_target_pairs={{0,1},{1,0},{2,3},{3,2},{4,5},{5,4},{6,7},{7,6},{8,9},{9,8},{10,11... | collective-permute-start | bytes 786440 | tf_op jit(solution)/shard_map/ppermute | solution.py:16
  48.0 12.5 %collective-permute-start.12 = (bf16[128,1024]{1,0:T(8,128)(2,1)S(1)}, bf16[128,1024]{1,0:T(8,128)(2,1)S(1)}, u32[]{:S(2)}, u32[]{:S(2)}) collective-permute-start(bf16[128,1024]{1,0:T(8,128)(2,1)S(1)} %fusion.49), channel_id=1, source_target_pairs={{0,1},{1,0},{2,3},{3,2},{4,5},{5,4},{6,7},{7,6},{8,9},{9,8},{10,11... | collective-permute-start | bytes 786440 | tf_op jit(solution)/shard_map/ppermute | solution.py:16
  48.6 12.0 %collective-permute-start.13 = (bf16[64,3584]{1,0:T(8,128)(2,1)S(1)}, bf16[64,3584]{1,0:T(8,128)(2,1)S(1)}, u32[]{:S(2)}, u32[]{:S(2)}) collective-permute-start(bf16[64,3584]{1,0:T(8,128)(2,1)S(1)} %pad_maximum_fusion.8), channel_id=1, source_target_pairs={{0,2},{2,0},{4,6},{6,4},{8,10},{10,8},{12,14},{14,12},{16,18},{18,... | collective-permute-start | bytes 1376264 | tf_op jit(solution)/shard_map/ppermute | solution.py:21
  63.2 9.3 %collective-permute-start.14 = (bf16[128,1024]{1,0:T(8,128)(2,1)S(1)}, bf16[128,1024]{1,0:T(8,128)(2,1)S(1)}, u32[]{:S(2)}, u32[]{:S(2)}) collective-permute-start(bf16[128,1024]{1,0:T(8,128)(2,1)S(1)} %fusion.34), channel_id=1, source_target_pairs={{0,1},{1,0},{2,3},{3,2},{4,5},{5,4},{6,7},{7,6},{8,9},{9,8},{10,11... | collective-permute-start | bytes 786440 | tf_op jit(solution)/shard_map/ppermute | solution.py:16
  67.2 9.1 %collective-permute-start.15 = (bf16[128,1024]{1,0:T(8,128)(2,1)S(1)}, bf16[128,1024]{1,0:T(8,128)(2,1)S(1)}, u32[]{:S(2)}, u32[]{:S(2)}) collective-permute-start(bf16[128,1024]{1,0:T(8,128)(2,1)S(1)} %fusion.37), channel_id=1, source_target_pairs={{0,1},{1,0},{2,3},{3,2},{4,5},{5,4},{6,7},{7,6},{8,9},{9,8},{10,11... | collective-permute-start | bytes 786440 | tf_op jit(solution)/shard_map/ppermute | solution.py:16
  77.1 5.6 %collective-permute-start.16 = (bf16[64,3584]{1,0:T(8,128)(2,1)S(1)}, bf16[64,3584]{1,0:T(8,128)(2,1)S(1)}, u32[]{:S(2)}, u32[]{:S(2)}) collective-permute-start(bf16[64,3584]{1,0:T(8,128)(2,1)S(1)} %slice.155), channel_id=1, source_target_pairs={{0,2},{2,0},{4,6},{6,4},{8,10},{10,8},{12,14},{14,12},{16,18},{18,... | collective-permute-start | bytes 1376264 | tf_op jit(solution)/shard_map/ppermute | solution.py:21
  82.8 8.1 %collective-permute-start.17 = (bf16[32,3584]{1,0:T(8,128)(2,1)S(1)}, bf16[32,3584]{1,0:T(8,128)(2,1)S(1)}, u32[]{:S(2)}, u32[]{:S(2)}) collective-permute-start(bf16[32,3584]{1,0:T(8,128)(2,1)S(1)} %slice.237), channel_id=1, source_target_pairs={{0,4},{2,6},{4,0},{6,2},{8,12},{10,14},{12,8},{14,10},{16,20},{18,... | collective-permute-start | bytes 688136 | tf_op jit(solution)/shard_map/ppermute | solution.py:21
  102.1 7.7 %collective-permute-start.21 = (bf16[64,3584]{1,0:T(8,128)(2,1)S(1)}, bf16[64,3584]{1,0:T(8,128)(2,1)S(1)}, u32[]{:S(2)}, u32[]{:S(2)}) collective-permute-start(bf16[64,3584]{1,0:T(8,128)(2,1)S(1)} %slice.160), channel_id=1, source_target_pairs={{0,2},{2,0},{4,6},{6,4},{8,10},{10,8},{12,14},{14,12},{16,18},{18,... | collective-permute-start | bytes 1376264 | tf_op jit(solution)/shard_map/ppermute | solution.py:21
  102.2 8.1 %collective-permute-start.18 = (bf16[8,3584]{1,0:T(8,128)(2,1)S(1)}, bf16[8,3584]{1,0:T(8,128)(2,1)S(1)}, u32[]{:S(2)}, u32[]{:S(2)}) collective-permute-start(bf16[8,3584]{1,0:T(8,128)(2,1)S(1)} %get-tuple-element.48), channel_id=1, source_target_pairs={{0,8},{2,10},{4,12},{6,14},{8,0},{10,2},{12,4},{14,6},{16,24},{18,... | collective-permute-start | bytes 172040 | tf_op jit(solution)/shard_map/ppermute | solution.py:21
  102.6 7.7 %collective-permute-start.20 = (bf16[8,3584]{1,0:T(8,128)(2,1)S(1)}, bf16[8,3584]{1,0:T(8,128)(2,1)S(1)}, u32[]{:S(2)}, u32[]{:S(2)}) collective-permute-start(bf16[8,3584]{1,0:T(8,128)(2,1)S(1)} %get-tuple-element.49), channel_id=1, source_target_pairs={{0,24},{2,26},{4,28},{6,30},{8,16},{10,18},{12,20},{14,22},{16,8},... | collective-permute-start | bytes 172040 | tf_op jit(solution)/shard_map/ppermute | solution.py:21
  104.0 7.6 %collective-permute-start.19 = (bf16[8,3584]{1,0:T(8,128)(2,1)S(1)}, bf16[8,3584]{1,0:T(8,128)(2,1)S(1)}, u32[]{:S(2)}, u32[]{:S(2)}) collective-permute-start(bf16[8,3584]{1,0:T(8,128)(2,1)S(1)} %get-tuple-element.50), channel_id=1, source_target_pairs={{0,16},{2,18},{4,20},{6,22},{8,24},{10,26},{12,28},{14,30},{16,0},... | collective-permute-start | bytes 172040 | tf_op jit(solution)/shard_map/ppermute | solution.py:21
  109.9 7.2 %collective-permute-start.22 = (bf16[32,3584]{1,0:T(8,128)(2,1)S(1)}, bf16[32,3584]{1,0:T(8,128)(2,1)S(1)}, u32[]{:S(2)}, u32[]{:S(2)}) collective-permute-start(bf16[32,3584]{1,0:T(8,128)(2,1)S(1)} %slice.236), channel_id=1, source_target_pairs={{0,4},{2,6},{4,0},{6,2},{8,12},{10,14},{12,8},{14,10},{16,20},{18,... | collective-permute-start | bytes 688136 | tf_op jit(solution)/shard_map/ppermute | solution.py:21
  117.2 11.6 %collective-permute-start.23 = (bf16[8,3584]{1,0:T(8,128)(2,1)S(1)}, bf16[8,3584]{1,0:T(8,128)(2,1)S(1)}, u32[]{:S(2)}, u32[]{:S(2)}) collective-permute-start(bf16[8,3584]{1,0:T(8,128)(2,1)S(1)} %get-tuple-element.45), channel_id=1, source_target_pairs={{0,8},{2,10},{4,12},{6,14},{8,0},{10,2},{12,4},{14,6},{16,24},{18,... | collective-permute-start | bytes 172040 | tf_op jit(solution)/shard_map/ppermute | solution.py:21
  118.6 10.3 %collective-permute-start.25 = (bf16[8,3584]{1,0:T(8,128)(2,1)S(1)}, bf16[8,3584]{1,0:T(8,128)(2,1)S(1)}, u32[]{:S(2)}, u32[]{:S(2)}) collective-permute-start(bf16[8,3584]{1,0:T(8,128)(2,1)S(1)} %get-tuple-element.46), channel_id=1, source_target_pairs={{0,24},{2,26},{4,28},{6,30},{8,16},{10,18},{12,20},{14,22},{16,8},... | collective-permute-start | bytes 172040 | tf_op jit(solution)/shard_map/ppermute | solution.py:21
  120.1 8.8 %collective-permute-start.24 = (bf16[8,3584]{1,0:T(8,128)(2,1)S(1)}, bf16[8,3584]{1,0:T(8,128)(2,1)S(1)}, u32[]{:S(2)}, u32[]{:S(2)}) collective-permute-start(bf16[8,3584]{1,0:T(8,128)(2,1)S(1)} %get-tuple-element.47), channel_id=1, source_target_pairs={{0,16},{2,18},{4,20},{6,22},{8,24},{10,26},{12,28},{14,30},{16,0},... | collective-permute-start | bytes 172040 | tf_op jit(solution)/shard_map/ppermute | solution.py:21

commit v3 on v2

v3 whole, which is shorter than its diff:
```python
import jax
import jax.numpy as jnp
from jax import lax
from jax.experimental import pallas as pl
from jax.experimental.pallas import tpu as pltpu
from jax.sharding import PartitionSpec as P

FF = 2048


def dp_sum(part, dp_count):
    sent = part.astype(jnp.bfloat16)
    if dp_count != 2:
        return lax.psum(sent, "dp").astype(jnp.float32)
    other = lax.ppermute(sent, "dp", [(0, 1), (1, 0)])
    return sent.astype(jnp.float32) + other.astype(jnp.float32)


def from_partner(block, offset, ep_count):
    return lax.ppermute(block, "ep", [(i, i ^ offset) for i in range(ep_count)])


def far_offsets(ep_count):
    return range(4, ep_count, 4)


def gather_far(block, ep_count):
    return jnp.concatenate(
        [block] + [from_partner(block, offset, ep_count) for offset in far_offsets(ep_count)]
    )


def gather_near(rows, ep_count):
    for offset in (2, 1):
        rows = jnp.concatenate([rows, from_partner(rows, offset, ep_count)])
    return rows


def sum_near(kept, offset, ep_count, beside):
    half = kept.shape[0] // 2
    sent, beside = lax.optimization_barrier((kept[half:].astype(jnp.bfloat16), beside))
    other = from_partner(sent, offset, ep_count)
    return (lambda: kept[:half].astype(jnp.float32) + other.astype(jnp.float32)), beside


def sum_far(kept, ep_count, beside):
    size = kept.shape[0] // (ep_count // 4)
    sent, beside = lax.optimization_barrier((kept.astype(jnp.bfloat16), beside))
    others = [
        from_partner(sent[number * size : (number + 1) * size], offset, ep_count)
        for number, offset in enumerate(far_offsets(ep_count), 1)
    ]

    def finish():
        total = kept[:size]
        for other in others:
            total = total + other.astype(jnp.float32)
        return total.astype(jnp.bfloat16)

    return finish, beside


def grad_kernel(x_ref, g_ref, *refs):
    o_ref = refs[-1]
    o_ref[...] = jnp.dot(
        x_ref[...], g_ref[...], preferred_element_type=jnp.float32
    ).astype(o_ref.dtype)


def grad_part(x_turned, pair, turn, start, count, block, whole):
    width, rows = x_turned.shape
    piece = pair.shape[1] // 2
    given = () if whole is None else (whole,)
    return pl.pallas_call(
        grad_kernel,
        out_shape=jax.ShapeDtypeStruct((width, 4 * piece), jnp.bfloat16),
        grid=(2, count),
        in_specs=[
            pl.BlockSpec((block, rows), lambda c, i: (i + start, 0)),
            pl.BlockSpec((rows, piece), lambda c, i: (0, c)),
        ]
        + [pl.BlockSpec(memory_space=pl.ANY)] * len(given),
        out_specs=pl.BlockSpec((block, piece), lambda c, i: (i + start, 2 * c + turn)),
        input_output_aliases={2: 0} if given else {},
        cost_estimate=pl.CostEstimate(
            flops=4 * count * block * rows * piece,
            bytes_accessed=4 * count * block * (piece + rows) + 4 * rows * piece,
            transcendentals=0,
        ),
        compiler_params=pltpu.CompilerParams(vmem_limit_bytes=32 * 2**20),
    )(x_turned, pair, *given)


def activate(gate, upper, grad_hidden):
    sigmoid_g = jax.nn.sigmoid(gate)
    silu_g = gate * sigmoid_g
    hidden = (silu_g * upper).astype(jnp.bfloat16)
    grad_gate = (grad_hidden * upper * sigmoid_g * (1.0 + gate * (1.0 - sigmoid_g))).astype(
        jnp.bfloat16
    )
    grad_up = (grad_hidden * silu_g).astype(jnp.bfloat16)
    return hidden, grad_gate, grad_up


def on_device(tokens, cotangent, routes, route_weights, gate_up, down_proj):
    tok_rows, width = tokens.shape
    hidden_units = down_proj.shape[1]
    split = FF // hidden_units
    ep_count = lax.axis_size("ep")
    dp_count = lax.axis_size("dp")
    experts = ep_count // split
    expert = lax.axis_index("ep") // split
    table = jnp.sum(
        jnp.where(
            routes[:, :, None] == jnp.arange(experts, dtype=jnp.int32)[None, None, :],
            route_weights[:, :, None],
            0.0,
        ),
        axis=1,
    )
    high = lax.reduce_precision(table, 8, 7)
    rest = table - high
    middle = lax.reduce_precision(rest, 8, 7)
    low = rest - middle
    packed = jnp.concatenate([high, middle, low], axis=1).astype(jnp.bfloat16)
    packed = jnp.pad(packed, ((0, 0), (0, -packed.shape[1] % 128)))
    first = gather_far(jnp.concatenate([tokens, packed], axis=1), ep_count)
    first, cotangent = lax.optimization_barrier((first, cotangent))
    first = gather_near(first, ep_count)
    d_far = gather_far(cotangent, ep_count)
    x_all = first[:, :width]
    parts = first[:, width:].astype(jnp.float32)
    mine = jnp.arange(experts, dtype=jnp.int32)[None, :] == expert
    weight = jnp.sum(
        jnp.where(
            mine,
            parts[:, :experts]
            + (parts[:, experts : 2 * experts] + parts[:, 2 * experts : 3 * experts]),
            0.0,
        ),
        axis=1,
        keepdims=True,
    )
    named = weight > 0.0
    x_rows = jnp.where(named, x_all, jnp.zeros_like(x_all))
    w_pair = gate_up[0]
    w_down = down_proj[0]
    piece = hidden_units // 2
    d_far, x_rows = lax.optimization_barrier((d_far, x_rows))
    d_near = jnp.concatenate([d_far, from_partner(d_far, 2, ep_count)])

    def pre_piece(at, x):
        return jnp.dot(
            x, w_pair[:, at : at + piece], preferred_element_type=jnp.float32
        ).astype(jnp.bfloat16)

    def back_piece(at, d):
        return lax.dot_general(
            d, w_down[at : at + piece], (((1,), (1,)), ((), ())), preferred_element_type=jnp.float32
        ).astype(jnp.bfloat16)

    gate_a = dp_sum(pre_piece(0, x_rows), dp_count)
    d_near, x_next = lax.optimization_barrier((d_near, x_rows))
    d_all = jnp.concatenate([d_near, from_partner(d_near, 1, ep_count)])
    upper_a = dp_sum(pre_piece(hidden_units, x_next), dp_count)
    d_rows = (weight * d_all.astype(jnp.float32)).astype(jnp.bfloat16)
    gate_a, x_next = lax.optimization_barrier((gate_a, x_next))
    gate_b = dp_sum(pre_piece(piece, x_next), dp_count)
    upper_a, d_rows = lax.optimization_barrier((upper_a, d_rows))
    back_a = dp_sum(back_piece(0, d_rows), dp_count)
    gate_b, x_next = lax.optimization_barrier((gate_b, x_next))
    upper_b = dp_sum(pre_piece(hidden_units + piece, x_next), dp_count)
    back_a, d_rows = lax.optimization_barrier((back_a, d_rows))
    last = back_piece(piece, d_rows)
    last, gate_a, upper_a, back_a = lax.optimization_barrier((last, gate_a, upper_a, back_a))
    back_b = dp_sum(last, dp_count)

    def dx_term(grad, at):
        return lax.dot_general(
            grad,
            w_pair[:, at : at + piece],
            (((1,), (1,)), ((), ())),
            preferred_element_type=jnp.float32,
        )

    block = 256 if width % 256 == 0 else width
    blocks = width // block
    x_turned = x_rows.T
    hidden_a, grad_gate, grad_up = activate(gate_a, upper_a, back_a)
    pair_a = jnp.concatenate([grad_gate, grad_up], axis=1)
    dx_sum = dx_term(grad_gate, 0) + dx_term(grad_up, hidden_units)
    out_sum = jnp.dot(hidden_a, w_down[:piece], preferred_element_type=jnp.float32)
    whole = None
    if blocks > 1:
        whole = grad_part(x_turned, pair_a, 0, 0, blocks // 2, block, whole)
    dx_sum, out_sum, gate_b, x_turned = lax.optimization_barrier(
        (dx_sum, out_sum, gate_b, x_turned)
    )
    hidden_b, grad_gate, grad_up = activate(gate_b, upper_b, back_b)
    pair_b = jnp.concatenate([grad_gate, grad_up], axis=1)
    out_sum = out_sum + jnp.dot(hidden_b, w_down[piece:], preferred_element_type=jnp.float32)
    out_rows = (weight * out_sum).astype(jnp.bfloat16)
    finish, grad_gate = sum_near(out_rows, 1, ep_count, grad_gate)
    dx_sum = dx_sum + dx_term(grad_gate, piece)
    finish, grad_up = sum_near(finish(), 2, ep_count, grad_up)
    dx_rows = (dx_sum + dx_term(grad_up, hidden_units + piece)).astype(jnp.bfloat16)
    finish_out, x_turned = sum_far(finish(), ep_count, x_turned)
    finish, x_turned = sum_near(dx_rows, 1, ep_count, x_turned)
    whole = grad_part(x_turned, pair_a, 0, blocks // 2, blocks - blocks // 2, block, whole)
    finish, x_turned = sum_near(finish(), 2, ep_count, x_turned)
    early = blocks * 3 // 7
    if early > 0:
        whole = grad_part(x_turned, pair_b, 1, 0, early, block, whole)
    finish, x_turned = sum_far(finish(), ep_count, x_turned)
    weight_grad = grad_part(x_turned, pair_b, 1, early, blocks - early, block, whole)
    mixed = finish_out()
    token_grad = finish()
    return (mixed, token_grad, weight_grad[None])


def solution(mesh):
    return jax.shard_map(
        on_device,
        mesh=mesh,
        in_specs=(
            P("ep", "dp"),
            P("ep", "dp"),
            P("ep", None),
            P("ep", None),
            P("ep", "dp", None),
            P("ep", None, "dp"),
        ),
        out_specs=(P("ep", "dp"), P("ep", "dp"), P("ep", "dp", None)),
        check_vma=False,
    )
```

time: 130 us -> 153 us (1.18)
  matrix products: 46.9 us -> 62.7 us
  waiting for transfers between devices: 28.6 us -> 13.6 us
  Pallas kernels: 16.8 us -> 31.7 us
  starting transfers between devices: 26.3 us -> 31.2 us
  other arithmetic: 8.36 us -> 11.2 us
    dot_general x7 -> x8, matrix products: 29.5 us -> 44.7 us  [the longest x4 21.7 us: dx_term(): lax.dot_general(grad, w_pair[:, at:at + piece], (((1,), (1,)), ((), ())),...]
    pallas_call x3 -> x4, Pallas kernels: 16.8 us -> 31.7 us  [grad_part(): pl.pallas_call(grad_kernel, out_shape=jax.ShapeDtypeStruct((width, 4 * pi...]
    ppermute x6, waiting for transfers between devices: 17.7 us -> 5.13 us  [dp_sum(): other = lax.ppermute(sent, 'dp', [(0, 1), (1, 0)])]
    ppermute x6, starting transfers between devices: 6.33 us -> 9.13 us  [dp_sum(): other = lax.ppermute(sent, 'dp', [(0, 1), (1, 0)])]
    ppermute x20, waiting for transfers between devices: 10.9 us -> 8.5 us  [from_partner(): return lax.ppermute(block, 'ep', [(i, i ^ offset) for i in range(ep_count)])]
    convert_element_type x1 -> x3, other arithmetic: 0.61 us -> 2.82 us  [the longest x2 2.6 us: activate(): grad_up = (grad_hidden * silu_g).astype(jnp.bfloat16)]
    ppermute x20, starting transfers between devices: 20 us -> 22.1 us  [from_partner(): return lax.ppermute(block, 'ep', [(i, i ^ offset) for i in range(ep_count)])]
  transfers between devices with their start and end apart: 26 -> 26, of which waited for: 13 -> 9; matrix products, arithmetic and copies ran while one was open for 28% -> 41% of each run, Pallas kernels for 13% -> 21%
where the time goes in v3:
time: 153 us
  matrix products  62.7 us (41%)
  Pallas kernels  31.7 us (21%)
  starting transfers between devices  31.2 us (20%)
  waiting for transfers between devices  13.6 us (9%)
  other arithmetic  11.2 us (7%)
  local copies, waits for them, and re-layouts  1.56 us (1%)
    pallas_call x4, Pallas kernels, grad_part(): pl.pallas_call(grad_kernel, out_shape=jax.ShapeDtypeStruct((width, 4 * pi...  31.7 us
    ppermute x20, starting transfers between devices, from_partner(): return lax.ppermute(block, 'ep', [(i, i ^ offset) for i in range(ep_count)])  22.1 us
    dot_general x4, matrix products, dx_term(): lax.dot_general(grad, w_pair[:, at:at + piece], (((1,), (1,)), ((), ())),...  21.7 us
    dot_general x4, matrix products, pre_piece(): jnp.dot(x, w_pair[:, at:at + piece], preferred_element_type=jnp.float32)  17.9 us
    dot_general x2, matrix products, back_piece(): lax.dot_general(d, w_down[at:at + piece], (((1,), (1,)), ((), ())), prefe...  12.3 us
    ppermute x6, starting transfers between devices, dp_sum(): other = lax.ppermute(sent, 'dp', [(0, 1), (1, 0)])  9.13 us
    ppermute x20, waiting for transfers between devices, from_partner(): return lax.ppermute(block, 'ep', [(i, i ^ offset) for i in range(ep_count)])  8.5 us
    dot_general x1, matrix products, on_device(): jnp.dot(hidden_a, w_down[:piece], preferred_element_type=jnp.float32)  5.64 us
  transfers between devices with their start and end apart: 26, of which 9 were waited for; matrix products, arithmetic and copies ran while one was open for 41% of the time, Pallas kernels for 21%

profile of v3, /device:TPU:0, one launch (start us, length us, event | category | flops | bytes accessed | tf_op | source)
XLA Modules:
  0.0 152.9 jit_solution(16267481791686373360)
XLA Ops:
  2.3 5.0 %collective-permute-start.2 = (bf16[8,3712]{1,0:T(8,128)(2,1)S(1)}, bf16[8,3712]{1,0:T(8,128)(2,1)S(1)}, u32[]{:S(2)}, u32[]{:S(2)}) collective-permute-start(bf16[8,3712]{1,0:T(8,128)(2,1)S(1)} %pad_maximum_fusion.8), channel_id=1, source_target_pairs={{0,24},{2,26},{4,28},{6,30},{8,16},{10,18},{12,20},{14,22},{16,8},... | collective-permute-start | bytes 178184 | tf_op jit(solution)/shard_map/ppermute | solution.py:20
  8.0 1.9 %collective-permute-done.2 = bf16[8,3712]{1,0:T(8,128)(2,1)S(1)} collective-permute-done((bf16[8,3712]{1,0:T(8,128)(2,1)S(1)}, bf16[8,3712]{1,0:T(8,128)(2,1)S(1)}, u32[]{:S(2)}, u32[]{:S(2)}) %collective-permute-start.2) | collective-permute-done | bytes 59424 | tf_op jit(solution)/shard_map/ppermute | solution.py:20
  9.8 2.7 %collective-permute-done.1 = bf16[8,3712]{1,0:T(8,128)(2,1)S(1)} collective-permute-done((bf16[8,3712]{1,0:T(8,128)(2,1)S(1)}, bf16[8,3712]{1,0:T(8,128)(2,1)S(1)}, u32[]{:S(2)}, u32[]{:S(2)}) %collective-permute-start.1) | collective-permute-done | bytes 59424 | tf_op jit(solution)/shard_map/ppermute | solution.py:20
  13.4 1.7 %collective-permute-start.3 = (bf16[32,3712]{1,0:T(8,128)(2,1)S(1)}, bf16[32,3712]{1,0:T(8,128)(2,1)S(1)}, u32[]{:S(2)}, u32[]{:S(2)}) collective-permute-start(bf16[32,3712]{1,0:T(8,128)(2,1)S(1)} %pad_maximum_fusion.6), channel_id=1, source_target_pairs={{0,4},{2,6},{4,0},{6,2},{8,12},{10,14},{12,8},{14,10},{16,20},{18,... | collective-permute-start | bytes 712712 | tf_op jit(solution)/shard_map/ppermute | solution.py:20
  15.1 2.5 %collective-permute-start.7 = (bf16[8,3584]{1,0:T(8,128)(2,1)}, bf16[8,3584]{1,0:T(8,128)(2,1)S(1)}, u32[]{:S(2)}, u32[]{:S(2)}) collective-permute-start(bf16[8,3584]{1,0:T(8,128)(2,1)} %param.7), channel_id=1, source_target_pairs={{0,24},{2,26},{4,28},{6,30},{8,16},{10,18},{12,20},{14,22},{16,8},... | collective-permute-start | bytes 172040 | tf_op jit(solution)/shard_map/ppermute | solution.py:20
  17.6 1.8 %collective-permute-start.5 = (bf16[8,3584]{1,0:T(8,128)(2,1)}, bf16[8,3584]{1,0:T(8,128)(2,1)S(1)}, u32[]{:S(2)}, u32[]{:S(2)}) collective-permute-start(bf16[8,3584]{1,0:T(8,128)(2,1)} %param.7), channel_id=1, source_target_pairs={{0,8},{2,10},{4,12},{6,14},{8,0},{10,2},{12,4},{14,6},{16,24},{18,... | collective-permute-start | bytes 172040 | tf_op jit(solution)/shard_map/ppermute | solution.py:20
  21.7 1.2 collective-permute-done.6
  26.9 4.3 %fusion.52 = bf16[128,1024]{1,0:T(8,128)(2,1)S(1)} fusion(bf16[128,3584]{0,1:T(8,128)(2,1)S(1)} %fusion.67, bf16[3584,4096]{1,0:T(8,128)(2,1)} %bitcast.38), kind=kOutput, calls=%fused_computation.37 | convolution fusion | flops 939655168 | bytes 8519680 | tf_op jit(solution)/shard_map/dot_general | solution.py:153
  31.2 1.5 %collective-permute-start.12 = (bf16[128,1024]{1,0:T(8,128)(2,1)S(1)}, bf16[128,1024]{1,0:T(8,128)(2,1)S(1)}, u32[]{:S(2)}, u32[]{:S(2)}) collective-permute-start(bf16[128,1024]{1,0:T(8,128)(2,1)S(1)} %fusion.52), channel_id=1, source_target_pairs={{0,1},{1,0},{2,3},{3,2},{4,5},{5,4},{6,7},{7,6},{8,9},{9,8},{10,11... | collective-permute-start | bytes 786440 | tf_op jit(solution)/shard_map/ppermute | solution.py:15
  33.0 4.3 %fusion.49 = bf16[128,1024]{1,0:T(8,128)(2,1)S(1)} fusion(bf16[128,3584]{0,1:T(8,128)(2,1)S(1)} %fusion.67, bf16[3584,4096]{1,0:T(8,128)(2,1)} %bitcast.39), kind=kOutput, calls=%fused_computation.36 | convolution fusion | flops 939655168 | bytes 8519680 | tf_op jit(solution)/shard_map/dot_general | solution.py:153
  37.2 1.6 %collective-permute-start.9 = (bf16[128,1024]{1,0:T(8,128)(2,1)S(1)}, bf16[128,1024]{1,0:T(8,128)(2,1)S(1)}, u32[]{:S(2)}, u32[]{:S(2)}) collective-permute-start(bf16[128,1024]{1,0:T(8,128)(2,1)S(1)} %fusion.49), channel_id=1, source_target_pairs={{0,1},{1,0},{2,3},{3,2},{4,5},{5,4},{6,7},{7,6},{8,9},{9,8},{10,11... | collective-permute-start | bytes 786440 | tf_op jit(solution)/shard_map/ppermute | solution.py:15
  39.4 4.4 %fusion.55 = bf16[128,1024]{1,0:T(8,128)(2,1)S(1)} fusion(bf16[128,3584]{0,1:T(8,128)(2,1)S(1)} %fusion.67, bf16[3584,4096]{1,0:T(8,128)(2,1)} %bitcast.40), kind=kOutput, calls=%fused_computation.38 | convolution fusion | flops 939655168 | bytes 8519680 | tf_op jit(solution)/shard_map/dot_general | solution.py:153
  43.8 2.5 %collective-permute-start.13 = (bf16[128,1024]{1,0:T(8,128)(2,1)S(1)}, bf16[128,1024]{1,0:T(8,128)(2,1)S(1)}, u32[]{:S(2)}, u32[]{:S(2)}) collective-permute-start(bf16[128,1024]{1,0:T(8,128)(2,1)S(1)} %fusion.55), channel_id=1, source_target_pairs={{0,1},{1,0},{2,3},{3,2},{4,5},{5,4},{6,7},{7,6},{8,9},{9,8},{10,11... | collective-permute-start | bytes 786440 | tf_op jit(solution)/shard_map/ppermute | solution.py:15
  46.4 4.7 %collective-permute-done.13 = bf16[128,1024]{1,0:T(8,128)(2,1)S(1)} collective-permute-done((bf16[128,1024]{1,0:T(8,128)(2,1)S(1)}, bf16[128,1024]{1,0:T(8,128)(2,1)S(1)}, u32[]{:S(2)}, u32[]{:S(2)}) %collective-permute-start.13) | collective-permute-done | bytes 262176 | tf_op jit(solution)/shard_map/ppermute | solution.py:15
  52.2 5.7 %fusion.61 = bf16[128,1024]{1,0:T(8,128)(2,1)S(1)} fusion(bf16[128,3584]{1,0:T(8,128)(2,1)S(1)} %multiply_convert_fusion, bf16[1,2048,3584]{2,1,0:T(8,128)(2,1)} %param.11), kind=kOutput, calls=%fused_computation.40 | convolution fusion | flops 939655168 | bytes 8519680 | tf_op jit(solution)/shard_map/dot_general | solution.py:158
  57.9 1.7 %collective-permute-start.11 = (bf16[128,1024]{1,0:T(8,128)(2,1)S(1)}, bf16[128,1024]{1,0:T(8,128)(2,1)S(1)}, u32[]{:S(2)}, u32[]{:S(2)}) collective-permute-start(bf16[128,1024]{1,0:T(8,128)(2,1)S(1)} %fusion.61), channel_id=1, source_target_pairs={{0,1},{1,0},{2,3},{3,2},{4,5},{5,4},{6,7},{7,6},{8,9},{9,8},{10,11... | collective-permute-start | bytes 786440 | tf_op jit(solution)/shard_map/ppermute | solution.py:15
  59.5 5.0 %fusion.58 = bf16[128,1024]{1,0:T(8,128)(2,1)} fusion(bf16[128,3584]{0,1:T(8,128)(2,1)S(1)} %fusion.67, bf16[3584,4096]{1,0:T(8,128)(2,1)} %bitcast.41), kind=kOutput, calls=%fused_computation.39 | convolution fusion | flops 939655168 | bytes 8519680 | tf_op jit(solution)/shard_map/dot_general | solution.py:153
  65.3 6.6 %fusion.64 = bf16[128,1024]{1,0:T(8,128)(2,1)} fusion(bf16[128,3584]{1,0:T(8,128)(2,1)S(1)} %multiply_convert_fusion, bf16[1,2048,3584]{2,1,0:T(8,128)(2,1)} %param.11), kind=kOutput, calls=%fused_computation.41 | convolution fusion | flops 939655168 | bytes 8519680 | tf_op jit(solution)/shard_map/dot_general | solution.py:158
  71.9 5.6 %fusion.4 = f32[128,3584]{1,0:T(8,128)} fusion(bf16[1,2048,3584]{2,1,0:T(8,128)(2,1)} %param.11, f32[128,1024]{1,0:T(8,128)S(1)} %convert_add_fusion.7, f32[128,1024]{1,0:T(8,128)S(1)} %convert_add_fusion.5), kind=kOutput, calls=%fused_computation.4 | convolution fusion | flops 940310528 | bytes 10223616 | tf_op jit(solution)/shard_map/dot_general | solution.py:192
  79.8 4.9 %fusion.16 = f32[128,3584]{1,0:T(8,128)} fusion(bf16[128,1024]{1,0:T(8,128)(2,1)} %get-tuple-element.78, bf16[3584,4096]{1,0:T(8,128)(2,1)S(1)} %bitcast.46), kind=kOutput, calls=%fused_computation.16 | convolution fusion | flops 939524096 | bytes 9437184 | tf_op jit(solution)/shard_map/dot_general | solution.py:179
  84.7 5.4 %fusion.28 = f32[128,3584]{1,0:T(8,128)} fusion(f32[128,3584]{1,0:T(8,128)} %fusion.16, bf16[128,1024]{1,0:T(8,128)(2,1)} %get-tuple-element.77, bf16[3584,4096]{1,0:T(8,128)(2,1)S(1)} %bitcast.47), kind=kOutput, calls=%fused_computation.28 | convolution fusion | flops 939982848 | bytes 11272192 | tf_op jit(solution)/shard_map/dot_general | solution.py:179
  90.1 5.2 %fusion.43 = bf16[128,3584]{1,0:T(8,128)(2,1)S(1)} fusion(f32[128,3584]{1,0:T(8,128)} %fusion.4, bf16[1,2048,3584]{2,1,0:T(8,128)(2,1)} %param.11, f32[128]{0:T(128)S(1)} %fusion.80, bf16[128,1024]{1,0:T(8,128)(2,1)} %collective-permute-done.14, bf16[128,1024]{1,0:T(8,128)(2,1)} %fusion.58, f32[128,1024]{1,0:T(8,128)} %convert_add_fusion.4), kind=kOutput, calls=%fused_computation.33 | convolution fusion | flops 942080000 | bytes 11141632 | tf_op jit(solution)/shard_map/dot_general | solution.py:201
  95.4 7.9 %shard_map.85.refs_0_ = bf16[3584,4096]{1,0:T(8,128)(2,1)} custom-call(bf16[3584,128]{1,0:T(8,128)(2,1)S(1)} %bitcast.33, bf16[128,2048]{1,0:T(8,128)(2,1)S(1)} %pad_maximum_fusion.3.g_ref), custom_call_target="tpu_custom_call" | custom-call | flops 939524096 | bytes 8781824 | tf_op jit(solution)/shard_map/pallas_call | solution.py:74
  103.3 1.5 %multiply_convert_fusion.1 = (bf16[128,1024]{1,0:T(8,128)(2,1)S(1)}, bf16[128,1024]{1,0:T(8,128)(2,1)S(1)}) fusion(bf16[128,1024]{1,0:T(8,128)(2,1)} %collective-permute-done.15, bf16[128,1024]{1,0:T(8,128)(2,1)} %fusion.64, f32[128,1024]{1,0:T(8,128)S(1)} %copy-done.2, bf16[128,1024]{1,0:T(8,128)(2,1)} %collective-permute-done.14, bf16[128,1024]{1,0:T(8,128)(2,1)} %fusion.58), kind=kLoop, calls=%fused_computation.49 | loop fusion | flops 2490368 | bytes 2097152 | tf_op jit(solution)/shard_map/convert_element_type | solution.py:101
  105.0 5.7 %fusion.31 = f32[128,3584]{1,0:T(8,128)S(1)} fusion(f32[128,3584]{1,0:T(8,128)S(1)} %copy-done, bf16[128,1024]{1,0:T(8,128)(2,1)S(1)} %get-tuple-element.62, bf16[3584,4096]{1,0:T(8,128)(2,1)} %bitcast.42), kind=kOutput, calls=%fused_computation.29 | convolution fusion | flops 939982848 | bytes 11272192 | tf_op jit(solution)/shard_map/dot_general | solution.py:179
  111.9 5.7 %fusion.46 = bf16[128,3584]{1,0:T(8,128)(2,1)S(1)} fusion(f32[128,3584]{1,0:T(8,128)S(1)} %fusion.31, bf16[128,1024]{1,0:T(8,128)(2,1)S(1)} %get-tuple-element.63, bf16[3584,4096]{1,0:T(8,128)(2,1)} %bitcast.43), kind=kOutput, calls=%fused_computation.34 | convolution fusion | flops 940441600 | bytes 10354688 | tf_op jit(solution)/shard_map/dot_general | solution.py:179
  117.6 1.3 collective-permute-done.17
  120.0 2.8 %collective-permute-start.20 = (bf16[8,3584]{1,0:T(8,128)(2,1)S(1)}, bf16[8,3584]{1,0:T(8,128)(2,1)S(1)}, u32[]{:S(2)}, u32[]{:S(2)}) collective-permute-start(bf16[8,3584]{1,0:T(8,128)(2,1)S(1)} %get-tuple-element.83), channel_id=1, source_target_pairs={{0,24},{2,26},{4,28},{6,30},{8,16},{10,18},{12,20},{14,22},{16,8},... | collective-permute-start | bytes 172040 | tf_op jit(solution)/shard_map/ppermute | solution.py:20
  122.8 7.9 %shard_map.86.refs_0_ = bf16[3584,4096]{1,0:T(8,128)(2,1)} custom-call(bf16[3584,128]{1,0:T(8,128)(2,1)S(1)} %bitcast.34, bf16[128,2048]{1,0:T(8,128)(2,1)S(1)} %pad_maximum_fusion.3.g_ref, bf16[3584,4096]{1,0:T(8,128)(2,1)} %shard_map.85.refs_0_), custom_call_target="tpu_custom_call", output_to_operand_aliasing={{}: (2, {})} | custom-call | flops 939524096 | bytes 8781824 | tf_op jit(solution)/shard_map/pallas_call | solution.py:74
  132.4 6.8 %shard_map.87.refs_0_ = bf16[3584,4096]{1,0:T(8,128)(2,1)} custom-call(bf16[3584,128]{1,0:T(8,128)(2,1)S(1)} %bitcast.35, bf16[128,2048]{1,0:T(8,128)(2,1)S(1)} %pad_maximum_fusion.2.g_ref, bf16[3584,4096]{1,0:T(8,128)(2,1)} %shard_map.86.refs_0_), custom_call_target="tpu_custom_call", output_to_operand_aliasing={{}: (2, {})} | custom-call | flops 805306368 | bytes 7602176 | tf_op jit(solution)/shard_map/pallas_call | solution.py:74
  140.4 2.8 %collective-permute-start.25 = (bf16[8,3584]{1,0:T(8,128)(2,1)S(1)}, bf16[8,3584]{1,0:T(8,128)(2,1)S(1)}, u32[]{:S(2)}, u32[]{:S(2)}) collective-permute-start(bf16[8,3584]{1,0:T(8,128)(2,1)S(1)} %get-tuple-element.80), channel_id=1, source_target_pairs={{0,24},{2,26},{4,28},{6,30},{8,16},{10,18},{12,20},{14,22},{16,8},... | collective-permute-start | bytes 172040 | tf_op jit(solution)/shard_map/ppermute | solution.py:20
  143.2 9.0 %shard_map.88 = bf16[3584,4096]{1,0:T(8,128)(2,1)} custom-call(bf16[3584,128]{1,0:T(8,128)(2,1)S(1)} %bitcast.36, bf16[128,2048]{1,0:T(8,128)(2,1)S(1)} %pad_maximum_fusion.2.g_ref, bf16[3584,4096]{1,0:T(8,128)(2,1)} %shard_map.87.refs_0_), custom_call_target="tpu_custom_call", output_to_operand_aliasing={{}: (2, {})} | custom-call | flops 1073741824 | bytes 9961472 | tf_op jit(solution)/shard_map/pallas_call | solution.py:74
  (95 shorter events, 20.1 us)
Async XLA Ops:
  2.3 7.5 %collective-permute-start.2 = (bf16[8,3712]{1,0:T(8,128)(2,1)S(1)}, bf16[8,3712]{1,0:T(8,128)(2,1)S(1)}, u32[]{:S(2)}, u32[]{:S(2)}) collective-permute-start(bf16[8,3712]{1,0:T(8,128)(2,1)S(1)} %pad_maximum_fusion.8), channel_id=1, source_target_pairs={{0,24},{2,26},{4,28},{6,30},{8,16},{10,18},{12,20},{14,22},{16,8},... | collective-permute-start | bytes 178184 | tf_op jit(solution)/shard_map/ppermute | solution.py:20
  7.4 5.2 %collective-permute-start.1 = (bf16[8,3712]{1,0:T(8,128)(2,1)S(1)}, bf16[8,3712]{1,0:T(8,128)(2,1)S(1)}, u32[]{:S(2)}, u32[]{:S(2)}) collective-permute-start(bf16[8,3712]{1,0:T(8,128)(2,1)S(1)} %pad_maximum_fusion.8), channel_id=1, source_target_pairs={{0,16},{2,18},{4,20},{6,22},{8,24},{10,26},{12,28},{14,30},{16,0},... | collective-permute-start | bytes 178184 | tf_op jit(solution)/shard_map/ppermute | solution.py:20
  7.4 5.2 %collective-permute-start = (bf16[8,3712]{1,0:T(8,128)(2,1)S(1)}, bf16[8,3712]{1,0:T(8,128)(2,1)S(1)}, u32[]{:S(2)}, u32[]{:S(2)}) collective-permute-start(bf16[8,3712]{1,0:T(8,128)(2,1)S(1)} %pad_maximum_fusion.8), channel_id=1, source_target_pairs={{0,8},{2,10},{4,12},{6,14},{8,0},{10,2},{12,4},{14,6},{16,24},{18,... | collective-permute-start | bytes 178184 | tf_op jit(solution)/shard_map/ppermute | solution.py:20
  13.4 6.9 %collective-permute-start.3 = (bf16[32,3712]{1,0:T(8,128)(2,1)S(1)}, bf16[32,3712]{1,0:T(8,128)(2,1)S(1)}, u32[]{:S(2)}, u32[]{:S(2)}) collective-permute-start(bf16[32,3712]{1,0:T(8,128)(2,1)S(1)} %pad_maximum_fusion.6), channel_id=1, source_target_pairs={{0,4},{2,6},{4,0},{6,2},{8,12},{10,14},{12,8},{14,10},{16,20},{18,... | collective-permute-start | bytes 712712 | tf_op jit(solution)/shard_map/ppermute | solution.py:20
  15.1 6.6 %collective-permute-start.7 = (bf16[8,3584]{1,0:T(8,128)(2,1)}, bf16[8,3584]{1,0:T(8,128)(2,1)S(1)}, u32[]{:S(2)}, u32[]{:S(2)}) collective-permute-start(bf16[8,3584]{1,0:T(8,128)(2,1)} %param.7), channel_id=1, source_target_pairs={{0,24},{2,26},{4,28},{6,30},{8,16},{10,18},{12,20},{14,22},{16,8},... | collective-permute-start | bytes 172040 | tf_op jit(solution)/shard_map/ppermute | solution.py:20
  17.6 5.3 %collective-permute-start.6 = (bf16[8,3584]{1,0:T(8,128)(2,1)}, bf16[8,3584]{1,0:T(8,128)(2,1)S(1)}, u32[]{:S(2)}, u32[]{:S(2)}) collective-permute-start(bf16[8,3584]{1,0:T(8,128)(2,1)} %param.7), channel_id=1, source_target_pairs={{0,16},{2,18},{4,20},{6,22},{8,24},{10,26},{12,28},{14,30},{16,0},... | collective-permute-start | bytes 172040 | tf_op jit(solution)/shard_map/ppermute | solution.py:20
  17.6 5.3 %collective-permute-start.5 = (bf16[8,3584]{1,0:T(8,128)(2,1)}, bf16[8,3584]{1,0:T(8,128)(2,1)S(1)}, u32[]{:S(2)}, u32[]{:S(2)}) collective-permute-start(bf16[8,3584]{1,0:T(8,128)(2,1)} %param.7), channel_id=1, source_target_pairs={{0,8},{2,10},{4,12},{6,14},{8,0},{10,2},{12,4},{14,6},{16,24},{18,... | collective-permute-start | bytes 172040 | tf_op jit(solution)/shard_map/ppermute | solution.py:20
  20.4 3.8 %collective-permute-start.4 = (bf16[64,3712]{1,0:T(8,128)(2,1)S(1)}, bf16[64,3712]{1,0:T(8,128)(2,1)S(1)}, u32[]{:S(2)}, u32[]{:S(2)}) collective-permute-start(bf16[64,3712]{1,0:T(8,128)(2,1)S(1)} %pad_maximum_fusion.4), channel_id=1, source_target_pairs={{0,2},{2,0},{4,6},{6,4},{8,10},{10,8},{12,14},{14,12},{16,18},{18,... | collective-permute-start | bytes 1425416 | tf_op jit(solution)/shard_map/ppermute | solution.py:20
  26.3 6.6 %collective-permute-start.8 = (bf16[32,3584]{1,0:T(8,128)(2,1)S(1)}, bf16[32,3584]{1,0:T(8,128)(2,1)S(1)}, u32[]{:S(2)}, u32[]{:S(2)}) collective-permute-start(bf16[32,3584]{1,0:T(8,128)(2,1)S(1)} %pad_maximum_fusion.7), channel_id=1, source_target_pairs={{0,4},{2,6},{4,0},{6,2},{8,12},{10,14},{12,8},{14,10},{16,20},{18,... | collective-permute-start | bytes 688136 | tf_op jit(solution)/shard_map/ppermute | solution.py:20
  31.2 8.1 %collective-permute-start.12 = (bf16[128,1024]{1,0:T(8,128)(2,1)S(1)}, bf16[128,1024]{1,0:T(8,128)(2,1)S(1)}, u32[]{:S(2)}, u32[]{:S(2)}) collective-permute-start(bf16[128,1024]{1,0:T(8,128)(2,1)S(1)} %fusion.52), channel_id=1, source_target_pairs={{0,1},{1,0},{2,3},{3,2},{4,5},{5,4},{6,7},{7,6},{8,9},{9,8},{10,11... | collective-permute-start | bytes 786440 | tf_op jit(solution)/shard_map/ppermute | solution.py:15
  37.2 9.0 %collective-permute-start.9 = (bf16[128,1024]{1,0:T(8,128)(2,1)S(1)}, bf16[128,1024]{1,0:T(8,128)(2,1)S(1)}, u32[]{:S(2)}, u32[]{:S(2)}) collective-permute-start(bf16[128,1024]{1,0:T(8,128)(2,1)S(1)} %fusion.49), channel_id=1, source_target_pairs={{0,1},{1,0},{2,3},{3,2},{4,5},{5,4},{6,7},{7,6},{8,9},{9,8},{10,11... | collective-permute-start | bytes 786440 | tf_op jit(solution)/shard_map/ppermute | solution.py:15
  39.4 40.4 %slice-start = ((s8[29360128]{0:T(1024)(128)(4,1)}), s8[4194304]{0:T(1024)(128)(4,1)S(1)}, s32[]{:S(2)}) async-start(s8[29360128]{0:T(1024)(128)(4,1)} %bitcast.44), calls=%async_computation | async-start | bytes 8388608
  39.4 40.3 %slice-start.1 = ((s8[29360128]{0:T(1024)(128)(4,1)}), s8[4194304]{0:T(1024)(128)(4,1)S(1)}, s32[]{:S(2)}) async-start(s8[29360128]{0:T(1024)(128)(4,1)} %bitcast.44), calls=%async_computation.1 | async-start | bytes 8388608
  43.8 7.3 %collective-permute-start.13 = (bf16[128,1024]{1,0:T(8,128)(2,1)S(1)}, bf16[128,1024]{1,0:T(8,128)(2,1)S(1)}, u32[]{:S(2)}, u32[]{:S(2)}) collective-permute-start(bf16[128,1024]{1,0:T(8,128)(2,1)S(1)} %fusion.55), channel_id=1, source_target_pairs={{0,1},{1,0},{2,3},{3,2},{4,5},{5,4},{6,7},{7,6},{8,9},{9,8},{10,11... | collective-permute-start | bytes 786440 | tf_op jit(solution)/shard_map/ppermute | solution.py:15
  46.3 5.7 %collective-permute-start.10 = (bf16[64,3584]{1,0:T(8,128)(2,1)S(1)}, bf16[64,3584]{1,0:T(8,128)(2,1)S(1)}, u32[]{:S(2)}, u32[]{:S(2)}) collective-permute-start(bf16[64,3584]{1,0:T(8,128)(2,1)S(1)} %pad_maximum_fusion.5), channel_id=1, source_target_pairs={{0,2},{2,0},{4,6},{6,4},{8,10},{10,8},{12,14},{14,12},{16,18},{18,... | collective-permute-start | bytes 1376264 | tf_op jit(solution)/shard_map/ppermute | solution.py:20
  52.2 27.6 %slice-start.2 = ((s8[29360128]{0:T(1024)(128)(4,1)}), s8[4194304]{0:T(1024)(128)(4,1)S(1)}, s32[]{:S(2)}) async-start(s8[29360128]{0:T(1024)(128)(4,1)} %bitcast.44), calls=%async_computation.2 | async-start | bytes 8388608
  57.9 21.9 %slice-start.3 = ((s8[29360128]{0:T(1024)(128)(4,1)}), s8[4194304]{0:T(1024)(128)(4,1)S(1)}, s32[]{:S(2)}) async-start(s8[29360128]{0:T(1024)(128)(4,1)} %bitcast.44), calls=%async_computation.3 | async-start | bytes 8388608
  57.9 7.3 %collective-permute-start.11 = (bf16[128,1024]{1,0:T(8,128)(2,1)S(1)}, bf16[128,1024]{1,0:T(8,128)(2,1)S(1)}, u32[]{:S(2)}, u32[]{:S(2)}) collective-permute-start(bf16[128,1024]{1,0:T(8,128)(2,1)S(1)} %fusion.61), channel_id=1, source_target_pairs={{0,1},{1,0},{2,3},{3,2},{4,5},{5,4},{6,7},{7,6},{8,9},{9,8},{10,11... | collective-permute-start | bytes 786440 | tf_op jit(solution)/shard_map/ppermute | solution.py:15
  64.5 15.2 %slice-start.4 = ((s8[29360128]{0:T(1024)(128)(4,1)}), s8[4194304]{0:T(1024)(128)(4,1)S(1)}, s32[]{:S(2)}) async-start(s8[29360128]{0:T(1024)(128)(4,1)} %bitcast.44), calls=%async_computation.4 | async-start | bytes 8388608
  64.5 25.6 %collective-permute-start.14 = (bf16[128,1024]{1,0:T(8,128)(2,1)}, bf16[128,1024]{1,0:T(8,128)(2,1)}, u32[]{:S(2)}, u32[]{:S(2)}) collective-permute-start(bf16[128,1024]{1,0:T(8,128)(2,1)} %fusion.58), channel_id=1, source_target_pairs={{0,1},{1,0},{2,3},{3,2},{4,5},{5,4},{6,7},{7,6},{8,9},{9,8},{10,11... | collective-permute-start | bytes 786440 | tf_op jit(solution)/shard_map/ppermute | solution.py:15
  65.3 14.5 %slice-start.5 = ((s8[29360128]{0:T(1024)(128)(4,1)}), s8[4194304]{0:T(1024)(128)(4,1)S(1)}, s32[]{:S(2)}) async-start(s8[29360128]{0:T(1024)(128)(4,1)} %bitcast.44), calls=%async_computation.5 | async-start | bytes 8388608
  78.6 24.7 %collective-permute-start.15 = (bf16[128,1024]{1,0:T(8,128)(2,1)}, bf16[128,1024]{1,0:T(8,128)(2,1)}, u32[]{:S(2)}, u32[]{:S(2)}) collective-permute-start(bf16[128,1024]{1,0:T(8,128)(2,1)} %fusion.64), channel_id=1, source_target_pairs={{0,1},{1,0},{2,3},{3,2},{4,5},{5,4},{6,7},{7,6},{8,9},{9,8},{10,11... | collective-permute-start | bytes 786440 | tf_op jit(solution)/shard_map/ppermute | solution.py:15
  104.9 5.8 %collective-permute-start.16 = (bf16[64,3584]{1,0:T(8,128)(2,1)S(1)}, bf16[64,3584]{1,0:T(8,128)(2,1)S(1)}, u32[]{:S(2)}, u32[]{:S(2)}) collective-permute-start(bf16[64,3584]{1,0:T(8,128)(2,1)S(1)} %slice.129), channel_id=1, source_target_pairs={{0,2},{2,0},{4,6},{6,4},{8,10},{10,8},{12,14},{14,12},{16,18},{18,... | collective-permute-start | bytes 1376264 | tf_op jit(solution)/shard_map/ppermute | solution.py:20
  110.8 8.1 %collective-permute-start.17 = (bf16[32,3584]{1,0:T(8,128)(2,1)S(1)}, bf16[32,3584]{1,0:T(8,128)(2,1)S(1)}, u32[]{:S(2)}, u32[]{:S(2)}) collective-permute-start(bf16[32,3584]{1,0:T(8,128)(2,1)S(1)} %slice.217), channel_id=1, source_target_pairs={{0,4},{2,6},{4,0},{6,2},{8,12},{10,14},{12,8},{14,10},{16,20},{18,... | collective-permute-start | bytes 688136 | tf_op jit(solution)/shard_map/ppermute | solution.py:20
  118.9 11.8 %collective-permute-start.21 = (bf16[64,3584]{1,0:T(8,128)(2,1)S(1)}, bf16[64,3584]{1,0:T(8,128)(2,1)S(1)}, u32[]{:S(2)}, u32[]{:S(2)}) collective-permute-start(bf16[64,3584]{1,0:T(8,128)(2,1)S(1)} %slice.134), channel_id=1, source_target_pairs={{0,2},{2,0},{4,6},{6,4},{8,10},{10,8},{12,14},{14,12},{16,18},{18,... | collective-permute-start | bytes 1376264 | tf_op jit(solution)/shard_map/ppermute | solution.py:20
  119.0 12.6 %collective-permute-start.18 = (bf16[8,3584]{1,0:T(8,128)(2,1)S(1)}, bf16[8,3584]{1,0:T(8,128)(2,1)S(1)}, u32[]{:S(2)}, u32[]{:S(2)}) collective-permute-start(bf16[8,3584]{1,0:T(8,128)(2,1)S(1)} %get-tuple-element.82), channel_id=1, source_target_pairs={{0,8},{2,10},{4,12},{6,14},{8,0},{10,2},{12,4},{14,6},{16,24},{18,... | collective-permute-start | bytes 172040 | tf_op jit(solution)/shard_map/ppermute | solution.py:20
  120.0 11.7 %collective-permute-start.20 = (bf16[8,3584]{1,0:T(8,128)(2,1)S(1)}, bf16[8,3584]{1,0:T(8,128)(2,1)S(1)}, u32[]{:S(2)}, u32[]{:S(2)}) collective-permute-start(bf16[8,3584]{1,0:T(8,128)(2,1)S(1)} %get-tuple-element.83), channel_id=1, source_target_pairs={{0,24},{2,26},{4,28},{6,30},{8,16},{10,18},{12,20},{14,22},{16,8},... | collective-permute-start | bytes 172040 | tf_op jit(solution)/shard_map/ppermute | solution.py:20
  122.8 8.9 %collective-permute-start.19 = (bf16[8,3584]{1,0:T(8,128)(2,1)S(1)}, bf16[8,3584]{1,0:T(8,128)(2,1)S(1)}, u32[]{:S(2)}, u32[]{:S(2)}) collective-permute-start(bf16[8,3584]{1,0:T(8,128)(2,1)S(1)} %get-tuple-element.84), channel_id=1, source_target_pairs={{0,16},{2,18},{4,20},{6,22},{8,24},{10,26},{12,28},{14,30},{16,0},... | collective-permute-start | bytes 172040 | tf_op jit(solution)/shard_map/ppermute | solution.py:20
  130.9 8.3 %collective-permute-start.22 = (bf16[32,3584]{1,0:T(8,128)(2,1)S(1)}, bf16[32,3584]{1,0:T(8,128)(2,1)S(1)}, u32[]{:S(2)}, u32[]{:S(2)}) collective-permute-start(bf16[32,3584]{1,0:T(8,128)(2,1)S(1)} %slice.216), channel_id=1, source_target_pairs={{0,4},{2,6},{4,0},{6,2},{8,12},{10,14},{12,8},{14,10},{16,20},{18,... | collective-permute-start | bytes 688136 | tf_op jit(solution)/shard_map/ppermute | solution.py:20
  139.3 13.0 %collective-permute-start.23 = (bf16[8,3584]{1,0:T(8,128)(2,1)S(1)}, bf16[8,3584]{1,0:T(8,128)(2,1)S(1)}, u32[]{:S(2)}, u32[]{:S(2)}) collective-permute-start(bf16[8,3584]{1,0:T(8,128)(2,1)S(1)} %get-tuple-element.79), channel_id=1, source_target_pairs={{0,8},{2,10},{4,12},{6,14},{8,0},{10,2},{12,4},{14,6},{16,24},{18,... | collective-permute-start | bytes 172040 | tf_op jit(solution)/shard_map/ppermute | solution.py:20
  140.4 11.8 %collective-permute-start.25 = (bf16[8,3584]{1,0:T(8,128)(2,1)S(1)}, bf16[8,3584]{1,0:T(8,128)(2,1)S(1)}, u32[]{:S(2)}, u32[]{:S(2)}) collective-permute-start(bf16[8,3584]{1,0:T(8,128)(2,1)S(1)} %get-tuple-element.80), channel_id=1, source_target_pairs={{0,24},{2,26},{4,28},{6,30},{8,16},{10,18},{12,20},{14,22},{16,8},... | collective-permute-start | bytes 172040 | tf_op jit(solution)/shard_map/ppermute | solution.py:20
  143.2 9.0 %collective-permute-start.24 = (bf16[8,3584]{1,0:T(8,128)(2,1)S(1)}, bf16[8,3584]{1,0:T(8,128)(2,1)S(1)}, u32[]{:S(2)}, u32[]{:S(2)}) collective-permute-start(bf16[8,3584]{1,0:T(8,128)(2,1)S(1)} %get-tuple-element.81), channel_id=1, source_target_pairs={{0,16},{2,18},{4,20},{6,22},{8,24},{10,26},{12,28},{14,30},{16,0},... | collective-permute-start | bytes 172040 | tf_op jit(solution)/shard_map/ppermute | solution.py:20
  (5 other events, 35.8 us)

commit v4 on v2

--- a/solution.py
+++ b/solution.py
@@ -181,7 +181,8 @@
     out_rows = (weight * jnp.dot(hidden, w_down, preferred_element_type=jnp.float32)).astype(
         jnp.bfloat16
     )
-    strip = width // 4 if width % 512 == 0 else width // 2
+    strip = width // 2
+    x_turned = x_rows.T
 
     def dx_strips(pair, begin, end):
         return [
@@ -197,15 +198,12 @@
     finish, pair = sum_near(out_rows, 1, ep_count, grad_pair)
     strips = dx_strips(pair, 0, strip)
     finish, pair = sum_near(finish(), 2, ep_count, pair)
-    strips += dx_strips(pair, strip, width // 2)
-    finish, pair = sum_far(finish(), ep_count, pair)
-    strips += dx_strips(pair, width // 2, width)
-    mixed = finish()
+    strips += dx_strips(pair, strip, width)
+    finish_out, x_turned = sum_far(finish(), ep_count, x_turned)
     dx_rows = jnp.concatenate(strips, axis=1)
     block = 256 if width % 256 == 0 else width
     blocks = width // block
     cuts = (0, blocks // 4, blocks * 9 // 16, blocks)
-    x_turned = x_rows.T
     whole = None
     finish, x_turned = sum_near(dx_rows, 1, ep_count, x_turned)
     for number in range(3):
@@ -216,6 +214,7 @@
             finish, x_turned = sum_near(finish(), 2, ep_count, x_turned)
         if number == 1:
             finish, x_turned = sum_far(finish(), ep_count, x_turned)
+    mixed = finish_out()
     token_grad = finish()
     weight_grad = whole
     return (mixed, token_grad, weight_grad[None])

time: 130 us -> 126 us (0.969)
  waiting for transfers between devices: 28.6 us -> 24.5 us
  starting transfers between devices: 26.3 us -> 28.3 us
  matrix products: 46.9 us -> 45.1 us
    ppermute x20, waiting for transfers between devices: 10.9 us -> 6.97 us  [from_partner(): return lax.ppermute(block, 'ep', [(i, i ^ offset) for i in range(ep_count)])]
    ppermute x20, starting transfers between devices: 20 us -> 21.9 us  [from_partner(): return lax.ppermute(block, 'ep', [(i, i ^ offset) for i in range(ep_count)])]
    dot_general x4 -> x2, matrix products: 22.1 us -> 20.2 us  [dx_strips(): lax.dot_general(pair, w_pair[at:at + strip], (((1,), (1,)), ((), ())), pr...]
  transfers between devices with their start and end apart: 26 -> 26, of which waited for: 13 -> 10; matrix products, arithmetic and copies ran while one was open for 28% -> 37% of each run, Pallas kernels for 13% -> 13%
where the time goes in v4:
time: 126 us
  matrix products  45.1 us (36%)
  starting transfers between devices  28.3 us (22%)
  waiting for transfers between devices  24.5 us (19%)
  Pallas kernels  16.8 us (13%)
  other arithmetic  8.28 us (7%)
  local copies, waits for them, and re-layouts  1.49 us (1%)
    ppermute x20, starting transfers between devices, from_partner(): return lax.ppermute(block, 'ep', [(i, i ^ offset) for i in range(ep_count)])  21.9 us
    dot_general x2, matrix products, dx_strips(): lax.dot_general(pair, w_pair[at:at + strip], (((1,), (1,)), ((), ())), pr...  20.2 us
    ppermute x6, waiting for transfers between devices, dp_sum(): other = lax.ppermute(sent, 'dp', [(0, 1), (1, 0)])  17.6 us
    dot_general x4, matrix products, pre_piece(): jnp.dot(x, w_pair[:, at:at + piece], preferred_element_type=jnp.float32)  17.5 us
    pallas_call x3, Pallas kernels, grad_part(): pl.pallas_call(grad_kernel, out_shape=jax.ShapeDtypeStruct((width, column...  16.8 us
    ppermute x20, waiting for transfers between devices, from_partner(): return lax.ppermute(block, 'ep', [(i, i ^ offset) for i in range(ep_count)])  6.97 us
    ppermute x6, starting transfers between devices, dp_sum(): other = lax.ppermute(sent, 'dp', [(0, 1), (1, 0)])  6.35 us
    dot_general x2, matrix products, on_device(): lax.dot_general(d_rows, w_down[at:at + piece], (((1,), (1,)), ((), ())),...  5.03 us
  transfers between devices with their start and end apart: 26, of which 10 were waited for; matrix products, arithmetic and copies ran while one was open for 37% of the time, Pallas kernels for 13%

profile of v4, /device:TPU:0, one launch (start us, length us, event | category | flops | bytes accessed | tf_op | source)
XLA Modules:
  0.0 125.5 jit_solution(7219919574634778080)
XLA Ops:
  2.3 5.0 %collective-permute-start.2 = (bf16[8,3712]{1,0:T(8,128)(2,1)S(1)}, bf16[8,3712]{1,0:T(8,128)(2,1)S(1)}, u32[]{:S(2)}, u32[]{:S(2)}) collective-permute-start(bf16[8,3712]{1,0:T(8,128)(2,1)S(1)} %pad_maximum_fusion.11), channel_id=1, source_target_pairs={{0,24},{2,26},{4,28},{6,30},{8,16},{10,18},{12,20},{14,22},{16,8},... | collective-permute-start | bytes 178184 | tf_op jit(solution)/shard_map/ppermute | solution.py:21
  8.0 1.9 %collective-permute-done.2 = bf16[8,3712]{1,0:T(8,128)(2,1)S(1)} collective-permute-done((bf16[8,3712]{1,0:T(8,128)(2,1)S(1)}, bf16[8,3712]{1,0:T(8,128)(2,1)S(1)}, u32[]{:S(2)}, u32[]{:S(2)}) %collective-permute-start.2) | collective-permute-done | bytes 59424 | tf_op jit(solution)/shard_map/ppermute | solution.py:21
  9.8 2.7 %collective-permute-done.1 = bf16[8,3712]{1,0:T(8,128)(2,1)S(1)} collective-permute-done((bf16[8,3712]{1,0:T(8,128)(2,1)S(1)}, bf16[8,3712]{1,0:T(8,128)(2,1)S(1)}, u32[]{:S(2)}, u32[]{:S(2)}) %collective-permute-start.1) | collective-permute-done | bytes 59424 | tf_op jit(solution)/shard_map/ppermute | solution.py:21
  13.4 1.7 %collective-permute-start.3 = (bf16[32,3712]{1,0:T(8,128)(2,1)S(1)}, bf16[32,3712]{1,0:T(8,128)(2,1)S(1)}, u32[]{:S(2)}, u32[]{:S(2)}) collective-permute-start(bf16[32,3712]{1,0:T(8,128)(2,1)S(1)} %pad_maximum_fusion.9), channel_id=1, source_target_pairs={{0,4},{2,6},{4,0},{6,2},{8,12},{10,14},{12,8},{14,10},{16,20},{18,... | collective-permute-start | bytes 712712 | tf_op jit(solution)/shard_map/ppermute | solution.py:21
  15.1 2.5 %collective-permute-start.7 = (bf16[8,3584]{1,0:T(8,128)(2,1)}, bf16[8,3584]{1,0:T(8,128)(2,1)S(1)}, u32[]{:S(2)}, u32[]{:S(2)}) collective-permute-start(bf16[8,3584]{1,0:T(8,128)(2,1)} %param.7), channel_id=1, source_target_pairs={{0,24},{2,26},{4,28},{6,30},{8,16},{10,18},{12,20},{14,22},{16,8},... | collective-permute-start | bytes 172040 | tf_op jit(solution)/shard_map/ppermute | solution.py:21
  17.6 1.8 %collective-permute-start.5 = (bf16[8,3584]{1,0:T(8,128)(2,1)}, bf16[8,3584]{1,0:T(8,128)(2,1)S(1)}, u32[]{:S(2)}, u32[]{:S(2)}) collective-permute-start(bf16[8,3584]{1,0:T(8,128)(2,1)} %param.7), channel_id=1, source_target_pairs={{0,8},{2,10},{4,12},{6,14},{8,0},{10,2},{12,4},{14,6},{16,24},{18,... | collective-permute-start | bytes 172040 | tf_op jit(solution)/shard_map/ppermute | solution.py:21
  21.7 1.2 collective-permute-done.6
  26.9 4.3 %fusion.43 = bf16[128,1024]{1,0:T(8,128)(2,1)S(1)} fusion(bf16[128,3584]{0,1:T(8,128)(2,1)S(1)} %fusion.53, bf16[3584,4096]{1,0:T(8,128)(2,1)} %bitcast.40), kind=kOutput, calls=%fused_computation.30 | convolution fusion | flops 939655168 | bytes 8519680 | tf_op jit(solution)/shard_map/dot_general | solution.py:147
  31.2 4.4 %fusion.40 = bf16[128,1024]{1,0:T(8,128)(2,1)S(1)} fusion(bf16[128,3584]{0,1:T(8,128)(2,1)S(1)} %fusion.53, bf16[3584,4096]{1,0:T(8,128)(2,1)} %bitcast.41), kind=kOutput, calls=%fused_computation.29 | convolution fusion | flops 939655168 | bytes 8519680 | tf_op jit(solution)/shard_map/dot_general | solution.py:147
  35.6 1.5 %collective-permute-start.8 = (bf16[128,1024]{1,0:T(8,128)(2,1)S(1)}, bf16[128,1024]{1,0:T(8,128)(2,1)S(1)}, u32[]{:S(2)}, u32[]{:S(2)}) collective-permute-start(bf16[128,1024]{1,0:T(8,128)(2,1)S(1)} %fusion.40), channel_id=1, source_target_pairs={{0,1},{1,0},{2,3},{3,2},{4,5},{5,4},{6,7},{7,6},{8,9},{9,8},{10,11... | collective-permute-start | bytes 786440 | tf_op jit(solution)/shard_map/ppermute | solution.py:16
  37.8 4.4 %fusion.49 = bf16[128,1024]{1,0:T(8,128)(2,1)S(1)} fusion(bf16[128,3584]{0,1:T(8,128)(2,1)S(1)} %fusion.53, bf16[3584,4096]{1,0:T(8,128)(2,1)} %bitcast.42), kind=kOutput, calls=%fused_computation.32 | convolution fusion | flops 939655168 | bytes 8519680 | tf_op jit(solution)/shard_map/dot_general | solution.py:147
  42.2 4.4 %fusion.46 = bf16[128,1024]{1,0:T(8,128)(2,1)S(1)} fusion(bf16[128,3584]{0,1:T(8,128)(2,1)S(1)} %fusion.53, bf16[3584,4096]{1,0:T(8,128)(2,1)} %bitcast.43), kind=kOutput, calls=%fused_computation.31 | convolution fusion | flops 939655168 | bytes 8519680 | tf_op jit(solution)/shard_map/dot_general | solution.py:147
  46.6 1.6 %collective-permute-start.11 = (bf16[128,1024]{1,0:T(8,128)(2,1)S(1)}, bf16[128,1024]{1,0:T(8,128)(2,1)S(1)}, u32[]{:S(2)}, u32[]{:S(2)}) collective-permute-start(bf16[128,1024]{1,0:T(8,128)(2,1)S(1)} %fusion.46), channel_id=1, source_target_pairs={{0,1},{1,0},{2,3},{3,2},{4,5},{5,4},{6,7},{7,6},{8,9},{9,8},{10,11... | collective-permute-start | bytes 786440 | tf_op jit(solution)/shard_map/ppermute | solution.py:16
  48.8 1.3 %collective-permute-done.9 = bf16[128,1024]{1,0:T(8,128)(2,1)S(1)} collective-permute-done((bf16[128,1024]{1,0:T(8,128)(2,1)S(1)}, bf16[128,1024]{1,0:T(8,128)(2,1)S(1)}, u32[]{:S(2)}, u32[]{:S(2)}) %collective-permute-start.9) | collective-permute-done | bytes 262176 | tf_op jit(solution)/shard_map/ppermute | solution.py:16
  50.1 5.8 %collective-permute-done.11 = bf16[128,1024]{1,0:T(8,128)(2,1)S(1)} collective-permute-done((bf16[128,1024]{1,0:T(8,128)(2,1)S(1)}, bf16[128,1024]{1,0:T(8,128)(2,1)S(1)}, u32[]{:S(2)}, u32[]{:S(2)}) %collective-permute-start.11) | collective-permute-done | bytes 262176 | tf_op jit(solution)/shard_map/ppermute | solution.py:16
  56.0 4.6 %collective-permute-done.12 = bf16[128,1024]{1,0:T(8,128)(2,1)S(1)} collective-permute-done((bf16[128,1024]{1,0:T(8,128)(2,1)S(1)}, bf16[128,1024]{1,0:T(8,128)(2,1)S(1)}, u32[]{:S(2)}, u32[]{:S(2)}) %collective-permute-start.12) | collective-permute-done | bytes 262176 | tf_op jit(solution)/shard_map/ppermute | solution.py:16
  60.7 2.5 %fusion.34 = bf16[128,1024]{1,0:T(8,128)(2,1)S(1)} fusion(bf16[1,2048,3584]{2,1,0:T(8,128)(2,1)S(1)} %bitcast.45, bf16[64,3584]{1,0:T(8,128)(2,1)S(1)} %collective-permute-done.13, bf16[64,3584]{1,0:T(8,128)(2,1)S(1)} %pad_maximum_fusion.8, f32[128]{0:T(128)S(1)} %fusion.63), kind=kOutput, calls=%fused_computation.27 | convolution fusion | flops 942407680 | bytes 8520192 | tf_op jit(solution)/shard_map/dot_general | solution.py:160
  63.2 1.6 %collective-permute-start.14 = (bf16[128,1024]{1,0:T(8,128)(2,1)S(1)}, bf16[128,1024]{1,0:T(8,128)(2,1)S(1)}, u32[]{:S(2)}, u32[]{:S(2)}) collective-permute-start(bf16[128,1024]{1,0:T(8,128)(2,1)S(1)} %fusion.34), channel_id=1, source_target_pairs={{0,1},{1,0},{2,3},{3,2},{4,5},{5,4},{6,7},{7,6},{8,9},{9,8},{10,11... | collective-permute-start | bytes 786440 | tf_op jit(solution)/shard_map/ppermute | solution.py:16
  64.8 2.5 %fusion.37 = bf16[128,1024]{1,0:T(8,128)(2,1)S(1)} fusion(bf16[1,2048,3584]{2,1,0:T(8,128)(2,1)S(1)} %bitcast.45, bf16[64,3584]{1,0:T(8,128)(2,1)S(1)} %collective-permute-done.13, bf16[64,3584]{1,0:T(8,128)(2,1)S(1)} %pad_maximum_fusion.8, f32[128]{0:T(128)S(1)} %fusion.63), kind=kOutput, calls=%fused_computation.28 | convolution fusion | flops 942407680 | bytes 8520192 | tf_op jit(solution)/shard_map/dot_general | solution.py:160
  67.9 2.4 %fusion.25 = bf16[128,3584]{1,0:T(8,128)(2,1)S(1)} fusion(bf16[1,2048,3584]{2,1,0:T(8,128)(2,1)S(1)} %bitcast.45, f32[128]{0:T(128)S(1)} %fusion.63, f32[128,1024]{1,0:T(8,128)S(1)} %convert_add_fusion.4, f32[128,1024]{1,0:T(8,128)S(1)} %convert_add_fusion.5, f32[128,1024]{1,0:T(8,128)S(1)} %convert_add_fusion.6, f32[128,1024]{1,0:T(8,128)S(1)} %convert_add_fusion.7), kind=kOutput, calls=%fused_computation.23 | convolution fusion | flops 1882062848 | bytes 17695232 | tf_op jit(solution)/shard_map/dot_general | solution.py:181
  70.4 2.0 %collective-permute-done.14 = bf16[128,1024]{1,0:T(8,128)(2,1)S(1)} collective-permute-done((bf16[128,1024]{1,0:T(8,128)(2,1)S(1)}, bf16[128,1024]{1,0:T(8,128)(2,1)S(1)}, u32[]{:S(2)}, u32[]{:S(2)}) %collective-permute-start.14) | collective-permute-done | bytes 262176 | tf_op jit(solution)/shard_map/ppermute | solution.py:16
  72.5 3.8 %collective-permute-done.15 = bf16[128,1024]{1,0:T(8,128)(2,1)S(1)} collective-permute-done((bf16[128,1024]{1,0:T(8,128)(2,1)S(1)}, bf16[128,1024]{1,0:T(8,128)(2,1)S(1)}, u32[]{:S(2)}, u32[]{:S(2)}) %collective-permute-start.15) | collective-permute-done | bytes 262176 | tf_op jit(solution)/shard_map/ppermute | solution.py:16
  77.1 10.1 %fusion.28 = bf16[128,1792]{1,0:T(8,128)(2,1)S(1)} fusion(bf16[128,4096]{1,0:T(8,128)(2,1)S(1)} %pad_maximum_fusion.3.g_ref, bf16[1,3584,4096]{2,1,0:T(8,128)(2,1)} %param.10), kind=kOutput, calls=%fused_computation.24 | convolution fusion | flops 1879277568 | bytes 16187392 | tf_op jit(solution)/shard_map/dot_general | solution.py:189
  87.5 10.1 %fusion.31 = bf16[128,1792]{1,0:T(8,128)(2,1)S(1)} fusion(bf16[128,4096]{1,0:T(8,128)(2,1)S(1)} %pad_maximum_fusion.3.g_ref, bf16[1,3584,4096]{2,1,0:T(8,128)(2,1)} %param.10), kind=kOutput, calls=%fused_computation.25 | convolution fusion | flops 1879277568 | bytes 16187392 | tf_op jit(solution)/shard_map/dot_general | solution.py:189
  98.7 1.5 %collective-permute-start.20 = (bf16[8,3584]{1,0:T(8,128)(2,1)S(1)}, bf16[8,3584]{1,0:T(8,128)(2,1)S(1)}, u32[]{:S(2)}, u32[]{:S(2)}) collective-permute-start(bf16[8,3584]{1,0:T(8,128)(2,1)S(1)} %get-tuple-element.49), channel_id=1, source_target_pairs={{0,24},{2,26},{4,28},{6,30},{8,16},{10,18},{12,20},{14,22},{16,8},... | collective-permute-start | bytes 172040 | tf_op jit(solution)/shard_map/ppermute | solution.py:21
  100.2 1.7 %collective-permute-start.19 = (bf16[8,3584]{1,0:T(8,128)(2,1)S(1)}, bf16[8,3584]{1,0:T(8,128)(2,1)S(1)}, u32[]{:S(2)}, u32[]{:S(2)}) collective-permute-start(bf16[8,3584]{1,0:T(8,128)(2,1)S(1)} %get-tuple-element.50), channel_id=1, source_target_pairs={{0,16},{2,18},{4,20},{6,22},{8,24},{10,26},{12,28},{14,30},{16,0},... | collective-permute-start | bytes 172040 | tf_op jit(solution)/shard_map/ppermute | solution.py:21
  101.8 4.0 %shard_map.85.refs_0_ = bf16[3584,4096]{1,0:T(8,128)(2,1)} custom-call(bf16[3584,128]{1,0:T(8,128)(2,1)S(1)} %bitcast.36, bf16[128,4096]{1,0:T(8,128)(2,1)S(1)} %pad_maximum_fusion.3.g_ref), custom_call_target="tpu_custom_call" | custom-call | flops 805306368 | bytes 7536640 | tf_op jit(solution)/shard_map/pallas_call | solution.py:78
  106.0 1.8 %collective-permute-start.22 = (bf16[32,3584]{1,0:T(8,128)(2,1)S(1)}, bf16[32,3584]{1,0:T(8,128)(2,1)S(1)}, u32[]{:S(2)}, u32[]{:S(2)}) collective-permute-start(bf16[32,3584]{1,0:T(8,128)(2,1)S(1)} %slice.215), channel_id=1, source_target_pairs={{0,4},{2,6},{4,0},{6,2},{8,12},{10,14},{12,8},{14,10},{16,20},{18,... | collective-permute-start | bytes 688136 | tf_op jit(solution)/shard_map/ppermute | solution.py:21
  108.5 4.7 %shard_map.86.refs_0_ = bf16[3584,4096]{1,0:T(8,128)(2,1)} custom-call(bf16[3584,128]{1,0:T(8,128)(2,1)S(1)} %bitcast.37, bf16[128,4096]{1,0:T(8,128)(2,1)S(1)} %pad_maximum_fusion.3.g_ref, bf16[3584,4096]{1,0:T(8,128)(2,1)} %shard_map.85.refs_0_), custom_call_target="tpu_custom_call", output_to_operand_aliasing={{}: (2, {})} | custom-call | flops 1073741824 | bytes 9699328 | tf_op jit(solution)/shard_map/pallas_call | solution.py:78
  113.3 1.3 %collective-permute-start.23 = (bf16[8,3584]{1,0:T(8,128)(2,1)S(1)}, bf16[8,3584]{1,0:T(8,128)(2,1)S(1)}, u32[]{:S(2)}, u32[]{:S(2)}) collective-permute-start(bf16[8,3584]{1,0:T(8,128)(2,1)S(1)} %get-tuple-element.45), channel_id=1, source_target_pairs={{0,8},{2,10},{4,12},{6,14},{8,0},{10,2},{12,4},{14,6},{16,24},{18,... | collective-permute-start | bytes 172040 | tf_op jit(solution)/shard_map/ppermute | solution.py:21
  114.5 1.4 %collective-permute-start.25 = (bf16[8,3584]{1,0:T(8,128)(2,1)S(1)}, bf16[8,3584]{1,0:T(8,128)(2,1)S(1)}, u32[]{:S(2)}, u32[]{:S(2)}) collective-permute-start(bf16[8,3584]{1,0:T(8,128)(2,1)S(1)} %get-tuple-element.46), channel_id=1, source_target_pairs={{0,24},{2,26},{4,28},{6,30},{8,16},{10,18},{12,20},{14,22},{16,8},... | collective-permute-start | bytes 172040 | tf_op jit(solution)/shard_map/ppermute | solution.py:21
  116.8 8.0 %shard_map.87 = bf16[3584,4096]{1,0:T(8,128)(2,1)} custom-call(bf16[3584,128]{1,0:T(8,128)(2,1)S(1)} %bitcast.38, bf16[128,4096]{1,0:T(8,128)(2,1)S(1)} %pad_maximum_fusion.3.g_ref, bf16[3584,4096]{1,0:T(8,128)(2,1)} %shard_map.86.refs_0_), custom_call_target="tpu_custom_call", output_to_operand_aliasing={{}: (2, {})} | custom-call | flops 1879048192 | bytes 16187392 | tf_op jit(solution)/shard_map/pallas_call | solution.py:78
  (76 shorter events, 15.8 us)
Async XLA Ops:
  2.3 7.5 %collective-permute-start.2 = (bf16[8,3712]{1,0:T(8,128)(2,1)S(1)}, bf16[8,3712]{1,0:T(8,128)(2,1)S(1)}, u32[]{:S(2)}, u32[]{:S(2)}) collective-permute-start(bf16[8,3712]{1,0:T(8,128)(2,1)S(1)} %pad_maximum_fusion.11), channel_id=1, source_target_pairs={{0,24},{2,26},{4,28},{6,30},{8,16},{10,18},{12,20},{14,22},{16,8},... | collective-permute-start | bytes 178184 | tf_op jit(solution)/shard_map/ppermute | solution.py:21
  7.4 5.2 %collective-permute-start.1 = (bf16[8,3712]{1,0:T(8,128)(2,1)S(1)}, bf16[8,3712]{1,0:T(8,128)(2,1)S(1)}, u32[]{:S(2)}, u32[]{:S(2)}) collective-permute-start(bf16[8,3712]{1,0:T(8,128)(2,1)S(1)} %pad_maximum_fusion.11), channel_id=1, source_target_pairs={{0,16},{2,18},{4,20},{6,22},{8,24},{10,26},{12,28},{14,30},{16,0},... | collective-permute-start | bytes 178184 | tf_op jit(solution)/shard_map/ppermute | solution.py:21
  7.4 5.2 %collective-permute-start = (bf16[8,3712]{1,0:T(8,128)(2,1)S(1)}, bf16[8,3712]{1,0:T(8,128)(2,1)S(1)}, u32[]{:S(2)}, u32[]{:S(2)}) collective-permute-start(bf16[8,3712]{1,0:T(8,128)(2,1)S(1)} %pad_maximum_fusion.11), channel_id=1, source_target_pairs={{0,8},{2,10},{4,12},{6,14},{8,0},{10,2},{12,4},{14,6},{16,24},{18,... | collective-permute-start | bytes 178184 | tf_op jit(solution)/shard_map/ppermute | solution.py:21
  13.4 6.9 %collective-permute-start.3 = (bf16[32,3712]{1,0:T(8,128)(2,1)S(1)}, bf16[32,3712]{1,0:T(8,128)(2,1)S(1)}, u32[]{:S(2)}, u32[]{:S(2)}) collective-permute-start(bf16[32,3712]{1,0:T(8,128)(2,1)S(1)} %pad_maximum_fusion.9), channel_id=1, source_target_pairs={{0,4},{2,6},{4,0},{6,2},{8,12},{10,14},{12,8},{14,10},{16,20},{18,... | collective-permute-start | bytes 712712 | tf_op jit(solution)/shard_map/ppermute | solution.py:21
  15.1 6.6 %collective-permute-start.7 = (bf16[8,3584]{1,0:T(8,128)(2,1)}, bf16[8,3584]{1,0:T(8,128)(2,1)S(1)}, u32[]{:S(2)}, u32[]{:S(2)}) collective-permute-start(bf16[8,3584]{1,0:T(8,128)(2,1)} %param.7), channel_id=1, source_target_pairs={{0,24},{2,26},{4,28},{6,30},{8,16},{10,18},{12,20},{14,22},{16,8},... | collective-permute-start | bytes 172040 | tf_op jit(solution)/shard_map/ppermute | solution.py:21
  17.6 5.3 %collective-permute-start.6 = (bf16[8,3584]{1,0:T(8,128)(2,1)}, bf16[8,3584]{1,0:T(8,128)(2,1)S(1)}, u32[]{:S(2)}, u32[]{:S(2)}) collective-permute-start(bf16[8,3584]{1,0:T(8,128)(2,1)} %param.7), channel_id=1, source_target_pairs={{0,16},{2,18},{4,20},{6,22},{8,24},{10,26},{12,28},{14,30},{16,0},... | collective-permute-start | bytes 172040 | tf_op jit(solution)/shard_map/ppermute | solution.py:21
  17.6 5.3 %collective-permute-start.5 = (bf16[8,3584]{1,0:T(8,128)(2,1)}, bf16[8,3584]{1,0:T(8,128)(2,1)S(1)}, u32[]{:S(2)}, u32[]{:S(2)}) collective-permute-start(bf16[8,3584]{1,0:T(8,128)(2,1)} %param.7), channel_id=1, source_target_pairs={{0,8},{2,10},{4,12},{6,14},{8,0},{10,2},{12,4},{14,6},{16,24},{18,... | collective-permute-start | bytes 172040 | tf_op jit(solution)/shard_map/ppermute | solution.py:21
  20.4 3.8 %collective-permute-start.4 = (bf16[64,3712]{1,0:T(8,128)(2,1)S(1)}, bf16[64,3712]{1,0:T(8,128)(2,1)S(1)}, u32[]{:S(2)}, u32[]{:S(2)}) collective-permute-start(bf16[64,3712]{1,0:T(8,128)(2,1)S(1)} %pad_maximum_fusion.6), channel_id=1, source_target_pairs={{0,2},{2,0},{4,6},{6,4},{8,10},{10,8},{12,14},{14,12},{16,18},{18,... | collective-permute-start | bytes 1425416 | tf_op jit(solution)/shard_map/ppermute | solution.py:21
  26.3 11.4 %collective-permute-start.10 = (bf16[32,3584]{1,0:T(8,128)(2,1)S(1)}, bf16[32,3584]{1,0:T(8,128)(2,1)S(1)}, u32[]{:S(2)}, u32[]{:S(2)}) collective-permute-start(bf16[32,3584]{1,0:T(8,128)(2,1)S(1)} %pad_maximum_fusion.10), channel_id=1, source_target_pairs={{0,4},{2,6},{4,0},{6,2},{8,12},{10,14},{12,8},{14,10},{16,20},{18,... | collective-permute-start | bytes 688136 | tf_op jit(solution)/shard_map/ppermute | solution.py:21
  31.2 29.5 %slice-start = ((s8[14680064]{0:T(1024)(128)(4,1)}), s8[4194304]{0:T(1024)(128)(4,1)S(1)}, s32[]{:S(2)}) async-start(s8[14680064]{0:T(1024)(128)(4,1)} %bitcast.44), calls=%async_computation | async-start | bytes 8388608
  31.2 29.5 %slice-start.1 = ((s8[14680064]{0:T(1024)(128)(4,1)}), s8[4194304]{0:T(1024)(128)(4,1)S(1)}, s32[]{:S(2)}) async-start(s8[14680064]{0:T(1024)(128)(4,1)} %bitcast.44), calls=%async_computation.1 | async-start | bytes 8388608
  35.6 13.1 %collective-permute-start.8 = (bf16[128,1024]{1,0:T(8,128)(2,1)S(1)}, bf16[128,1024]{1,0:T(8,128)(2,1)S(1)}, u32[]{:S(2)}, u32[]{:S(2)}) collective-permute-start(bf16[128,1024]{1,0:T(8,128)(2,1)S(1)} %fusion.40), channel_id=1, source_target_pairs={{0,1},{1,0},{2,3},{3,2},{4,5},{5,4},{6,7},{7,6},{8,9},{9,8},{10,11... | collective-permute-start | bytes 786440 | tf_op jit(solution)/shard_map/ppermute | solution.py:16
  37.2 12.9 %collective-permute-start.9 = (bf16[128,1024]{1,0:T(8,128)(2,1)S(1)}, bf16[128,1024]{1,0:T(8,128)(2,1)S(1)}, u32[]{:S(2)}, u32[]{:S(2)}) collective-permute-start(bf16[128,1024]{1,0:T(8,128)(2,1)S(1)} %fusion.43), channel_id=1, source_target_pairs={{0,1},{1,0},{2,3},{3,2},{4,5},{5,4},{6,7},{7,6},{8,9},{9,8},{10,11... | collective-permute-start | bytes 786440 | tf_op jit(solution)/shard_map/ppermute | solution.py:16
  37.7 22.9 %slice-start.2 = ((s8[14680064]{0:T(1024)(128)(4,1)}), s8[4194304]{0:T(1024)(128)(4,1)S(1)}, s32[]{:S(2)}) async-start(s8[14680064]{0:T(1024)(128)(4,1)} %bitcast.44), calls=%async_computation.2 | async-start | bytes 8388608
  42.2 18.5 %slice-start.3 = ((s8[14680064]{0:T(1024)(128)(4,1)}), s8[2097152]{0:T(1024)(128)(4,1)S(1)}, s32[]{:S(2)}) async-start(s8[14680064]{0:T(1024)(128)(4,1)} %bitcast.44), calls=%async_computation.3 | async-start | bytes 4194304
  46.6 9.3 %collective-permute-start.11 = (bf16[128,1024]{1,0:T(8,128)(2,1)S(1)}, bf16[128,1024]{1,0:T(8,128)(2,1)S(1)}, u32[]{:S(2)}, u32[]{:S(2)}) collective-permute-start(bf16[128,1024]{1,0:T(8,128)(2,1)S(1)} %fusion.46), channel_id=1, source_target_pairs={{0,1},{1,0},{2,3},{3,2},{4,5},{5,4},{6,7},{7,6},{8,9},{9,8},{10,11... | collective-permute-start | bytes 786440 | tf_op jit(solution)/shard_map/ppermute | solution.py:16
  48.2 12.4 %collective-permute-start.12 = (bf16[128,1024]{1,0:T(8,128)(2,1)S(1)}, bf16[128,1024]{1,0:T(8,128)(2,1)S(1)}, u32[]{:S(2)}, u32[]{:S(2)}) collective-permute-start(bf16[128,1024]{1,0:T(8,128)(2,1)S(1)} %fusion.49), channel_id=1, source_target_pairs={{0,1},{1,0},{2,3},{3,2},{4,5},{5,4},{6,7},{7,6},{8,9},{9,8},{10,11... | collective-permute-start | bytes 786440 | tf_op jit(solution)/shard_map/ppermute | solution.py:16
  48.7 12.0 %collective-permute-start.13 = (bf16[64,3584]{1,0:T(8,128)(2,1)S(1)}, bf16[64,3584]{1,0:T(8,128)(2,1)S(1)}, u32[]{:S(2)}, u32[]{:S(2)}) collective-permute-start(bf16[64,3584]{1,0:T(8,128)(2,1)S(1)} %pad_maximum_fusion.8), channel_id=1, source_target_pairs={{0,2},{2,0},{4,6},{6,4},{8,10},{10,8},{12,14},{14,12},{16,18},{18,... | collective-permute-start | bytes 1376264 | tf_op jit(solution)/shard_map/ppermute | solution.py:21
  63.2 9.2 %collective-permute-start.14 = (bf16[128,1024]{1,0:T(8,128)(2,1)S(1)}, bf16[128,1024]{1,0:T(8,128)(2,1)S(1)}, u32[]{:S(2)}, u32[]{:S(2)}) collective-permute-start(bf16[128,1024]{1,0:T(8,128)(2,1)S(1)} %fusion.34), channel_id=1, source_target_pairs={{0,1},{1,0},{2,3},{3,2},{4,5},{5,4},{6,7},{7,6},{8,9},{9,8},{10,11... | collective-permute-start | bytes 786440 | tf_op jit(solution)/shard_map/ppermute | solution.py:16
  67.3 9.0 %collective-permute-start.15 = (bf16[128,1024]{1,0:T(8,128)(2,1)S(1)}, bf16[128,1024]{1,0:T(8,128)(2,1)S(1)}, u32[]{:S(2)}, u32[]{:S(2)}) collective-permute-start(bf16[128,1024]{1,0:T(8,128)(2,1)S(1)} %fusion.37), channel_id=1, source_target_pairs={{0,1},{1,0},{2,3},{3,2},{4,5},{5,4},{6,7},{7,6},{8,9},{9,8},{10,11... | collective-permute-start | bytes 786440 | tf_op jit(solution)/shard_map/ppermute | solution.py:16
  77.0 10.2 %collective-permute-start.16 = (bf16[64,3584]{1,0:T(8,128)(2,1)S(1)}, bf16[64,3584]{1,0:T(8,128)(2,1)S(1)}, u32[]{:S(2)}, u32[]{:S(2)}) collective-permute-start(bf16[64,3584]{1,0:T(8,128)(2,1)S(1)} %slice.139), channel_id=1, source_target_pairs={{0,2},{2,0},{4,6},{6,4},{8,10},{10,8},{12,14},{14,12},{16,18},{18,... | collective-permute-start | bytes 1376264 | tf_op jit(solution)/shard_map/ppermute | solution.py:21
  87.4 10.3 %collective-permute-start.17 = (bf16[32,3584]{1,0:T(8,128)(2,1)S(1)}, bf16[32,3584]{1,0:T(8,128)(2,1)S(1)}, u32[]{:S(2)}, u32[]{:S(2)}) collective-permute-start(bf16[32,3584]{1,0:T(8,128)(2,1)S(1)} %slice.216), channel_id=1, source_target_pairs={{0,4},{2,6},{4,0},{6,2},{8,12},{10,14},{12,8},{14,10},{16,20},{18,... | collective-permute-start | bytes 688136 | tf_op jit(solution)/shard_map/ppermute | solution.py:21
  97.7 8.2 %collective-permute-start.21 = (bf16[64,3584]{1,0:T(8,128)(2,1)S(1)}, bf16[64,3584]{1,0:T(8,128)(2,1)S(1)}, u32[]{:S(2)}, u32[]{:S(2)}) collective-permute-start(bf16[64,3584]{1,0:T(8,128)(2,1)S(1)} %pad_maximum_fusion.7), channel_id=1, source_target_pairs={{0,2},{2,0},{4,6},{6,4},{8,10},{10,8},{12,14},{14,12},{16,18},{18,... | collective-permute-start | bytes 1376264 | tf_op jit(solution)/shard_map/ppermute | solution.py:21
  98.3 9.5 %collective-permute-start.18 = (bf16[8,3584]{1,0:T(8,128)(2,1)S(1)}, bf16[8,3584]{1,0:T(8,128)(2,1)S(1)}, u32[]{:S(2)}, u32[]{:S(2)}) collective-permute-start(bf16[8,3584]{1,0:T(8,128)(2,1)S(1)} %get-tuple-element.48), channel_id=1, source_target_pairs={{0,8},{2,10},{4,12},{6,14},{8,0},{10,2},{12,4},{14,6},{16,24},{18,... | collective-permute-start | bytes 172040 | tf_op jit(solution)/shard_map/ppermute | solution.py:21
  98.7 9.1 %collective-permute-start.20 = (bf16[8,3584]{1,0:T(8,128)(2,1)S(1)}, bf16[8,3584]{1,0:T(8,128)(2,1)S(1)}, u32[]{:S(2)}, u32[]{:S(2)}) collective-permute-start(bf16[8,3584]{1,0:T(8,128)(2,1)S(1)} %get-tuple-element.49), channel_id=1, source_target_pairs={{0,24},{2,26},{4,28},{6,30},{8,16},{10,18},{12,20},{14,22},{16,8},... | collective-permute-start | bytes 172040 | tf_op jit(solution)/shard_map/ppermute | solution.py:21
  100.2 7.6 %collective-permute-start.19 = (bf16[8,3584]{1,0:T(8,128)(2,1)S(1)}, bf16[8,3584]{1,0:T(8,128)(2,1)S(1)}, u32[]{:S(2)}, u32[]{:S(2)}) collective-permute-start(bf16[8,3584]{1,0:T(8,128)(2,1)S(1)} %get-tuple-element.50), channel_id=1, source_target_pairs={{0,16},{2,18},{4,20},{6,22},{8,24},{10,26},{12,28},{14,30},{16,0},... | collective-permute-start | bytes 172040 | tf_op jit(solution)/shard_map/ppermute | solution.py:21
  106.0 7.2 %collective-permute-start.22 = (bf16[32,3584]{1,0:T(8,128)(2,1)S(1)}, bf16[32,3584]{1,0:T(8,128)(2,1)S(1)}, u32[]{:S(2)}, u32[]{:S(2)}) collective-permute-start(bf16[32,3584]{1,0:T(8,128)(2,1)S(1)} %slice.215), channel_id=1, source_target_pairs={{0,4},{2,6},{4,0},{6,2},{8,12},{10,14},{12,8},{14,10},{16,20},{18,... | collective-permute-start | bytes 688136 | tf_op jit(solution)/shard_map/ppermute | solution.py:21
  113.3 11.6 %collective-permute-start.23 = (bf16[8,3584]{1,0:T(8,128)(2,1)S(1)}, bf16[8,3584]{1,0:T(8,128)(2,1)S(1)}, u32[]{:S(2)}, u32[]{:S(2)}) collective-permute-start(bf16[8,3584]{1,0:T(8,128)(2,1)S(1)} %get-tuple-element.45), channel_id=1, source_target_pairs={{0,8},{2,10},{4,12},{6,14},{8,0},{10,2},{12,4},{14,6},{16,24},{18,... | collective-permute-start | bytes 172040 | tf_op jit(solution)/shard_map/ppermute | solution.py:21
  114.5 10.3 %collective-permute-start.25 = (bf16[8,3584]{1,0:T(8,128)(2,1)S(1)}, bf16[8,3584]{1,0:T(8,128)(2,1)S(1)}, u32[]{:S(2)}, u32[]{:S(2)}) collective-permute-start(bf16[8,3584]{1,0:T(8,128)(2,1)S(1)} %get-tuple-element.46), channel_id=1, source_target_pairs={{0,24},{2,26},{4,28},{6,30},{8,16},{10,18},{12,20},{14,22},{16,8},... | collective-permute-start | bytes 172040 | tf_op jit(solution)/shard_map/ppermute | solution.py:21
  115.9 8.9 %collective-permute-start.24 = (bf16[8,3584]{1,0:T(8,128)(2,1)S(1)}, bf16[8,3584]{1,0:T(8,128)(2,1)S(1)}, u32[]{:S(2)}, u32[]{:S(2)}) collective-permute-start(bf16[8,3584]{1,0:T(8,128)(2,1)S(1)} %get-tuple-element.47), channel_id=1, source_target_pairs={{0,16},{2,18},{4,20},{6,22},{8,24},{10,26},{12,28},{14,30},{16,0},... | collective-permute-start | bytes 172040 | tf_op jit(solution)/shard_map/ppermute | solution.py:21
